TPU v7x, 128 devices: a whole 4x4x4 slice. The times are simulated.
128 devices in a mesh: patch: 128 (over z, x, y, core).
Axes of the slice: x: 4, y: 4, z: 4, core: 2. Of those that a mesh axis runs over, the one named last changes fastest.
Arguments:
- fine_nodes: float32 [32768, 512], P('patch'), may hold values from -6 to 6
- coarse_nodes: float32 [642, 512], replicated, may hold values from -6 to 6
- edge_feats: float32 [131072, 512], P('patch'), may hold values from -6 to 6
- senders: int32 [131072], P('patch'), may hold values from 0 to 1921, as said below
- receivers: int32 [131072], P('patch'), may hold values from 0 to 897, as said below
- send_rows: int32 [128, 128, 8], P('patch'), may hold values from 0 to 255
- w_edge_in: float32 [1536, 512], replicated, may hold values from -0.15625 to 0.15625
- w_edge_out: float32 [512, 512], replicated, may hold values from -0.25 to 0.25
- w_node_in: float32 [1024, 512], replicated, may hold values from -0.1875 to 0.1875
- w_node_out: float32 [512, 512], replicated, may hold values from -0.25 to 0.25
- cot_fine: float32 [32768, 512], P('patch'), may hold values from -6 to 6
- cot_coarse: float32 [642, 512], replicated, may hold values from -6 to 6
- cot_edges: float32 [131072, 512], P('patch'), may hold values from -6 to 6
Outputs:
- grad_fine: float32 [32768, 512], P('patch')
- grad_coarse: float32 [642, 512], replicated
- grad_edges: float32 [131072, 512], P('patch')
- grad_edge_in: float32 [1536, 512], replicated
- grad_edge_out: float32 [512, 512], replicated
- grad_node_in: float32 [1024, 512], replicated
- grad_node_out: float32 [512, 512], replicated
Inputs may be any that keep to these rules, and one draw needn't show every extreme that they name: Each patch's senders index its node table: its 256 fine nodes, then the 642 coarse nodes, then 8 halo rows from each patch in patch order; halo rows may come from any patch. Each patch's receivers index its own fine nodes, then the coarse nodes.
All inputs are finite; a program needn't handle non-finite values.
Results may differ from a plain program's by a relative error of at most 0.000076.
Values sent between devices are 32-bit elements; how exact they have to be, the bound alone decides.
A program may use at most 192 MiB of HBM per device.

v0:
```python
import functools
import math

import jax
import jax.numpy as jnp
from jax import lax
from jax.experimental import pallas as pl
from jax.experimental.pallas import tpu as pltpu
from jax.sharding import PartitionSpec as P

MESH = pl.DeviceIdType.MESH
F32 = jnp.float32
BF16 = jnp.bfloat16
FEAT = 512
FINE = 256
COARSE = 642
NEAR = 1024
EDGE = 1024
BLOCK = 256
LINKS = 6
LOCAL_BYTES = 30 << 20
FRONT_MIB, BACK_MIB, SUM_MIB = 36, 40, 40

NN = (((1,), (0,)), ((), ()))
NT = (((1,), (1,)), ((), ()))
TN = (((0,), (0,)), ((), ()))


def split(value):
    high = value.astype(BF16)
    return high, (value - high.astype(F32)).astype(BF16)


def dot(left, right, dims=NN):
    return lax.dot_general(left, right, dims, preferred_element_type=F32)


def dot3(left, right, dims=NN):
    return dot(left[0], right[0], dims) + dot(left[0], right[1], dims) + dot(left[1], right[0], dims)


def dot2(left, right, dims=NN):
    return dot(left, right[0], dims) + dot(left, right[1], dims)


def block_at(step):
    return pl.ds(pl.multiple_of(step * BLOCK, BLOCK), BLOCK)


def pair_at(refs, rows):
    return refs[0][rows, :], refs[1][rows, :]


def put_pair(refs, rows, value):
    high, low = split(value)
    refs[0][rows, :] = high
    refs[1][rows, :] = low


def spread(index_row):
    return jnp.transpose(jnp.broadcast_to(index_row, (128, index_row.shape[1])))


def hot_rows(spread_block, first, width):
    lane = lax.broadcasted_iota(jnp.int32, (spread_block.shape[0], 128), 1)
    local = spread_block - first
    tiles = [jnp.where(local == lane + at, 1.0, 0.0).astype(BF16) for at in range(0, width, 128)]
    return jnp.concatenate(tiles, axis=1)


def hot_columns(index_row, first, height):
    row = lax.broadcasted_iota(jnp.int32, (height, index_row.shape[1]), 0) + first
    return jnp.where(row == index_row, 1.0, 0.0).astype(BF16)


def sigmoid(value):
    return 1.0 / (1.0 + jnp.exp(-value))


def mean(value):
    return jnp.sum(value, axis=1, keepdims=True) * (1.0 / FEAT)


def norm(value):
    center = value - mean(value)
    scale = lax.rsqrt(mean(center * center) + 1e-05)
    return center * scale, scale


def norm_back(grad, normed, scale):
    return scale * (grad - mean(grad) - normed * mean(grad * normed))


def put_tiles(ref, value):
    for at in range(FEAT // 128):
        ref[:, at] = value[:, at * 128 : (at + 1) * 128].reshape(-1, 8, 128)


def vmem_specs(count):
    return [pl.BlockSpec(memory_space=pltpu.VMEM)] * count


def local_call(kernel, outs, scratch, flops, *args):
    moved = sum(math.prod(a.shape) * 4 for a in args) + sum(math.prod(o.shape) * 4 for o in outs)
    return pl.pallas_call(
        kernel,
        out_shape=outs,
        in_specs=vmem_specs(len(args)),
        out_specs=vmem_specs(len(outs)),
        scratch_shapes=scratch,
        compiler_params=pltpu.CompilerParams(vmem_limit_bytes=LOCAL_BYTES),
        cost_estimate=pl.CostEstimate(flops=int(flops), bytes_accessed=moved, transcendentals=0),
    )(*args)


def f32_out(*shape):
    return jax.ShapeDtypeStruct(shape, F32)


def bf16_out(*shape):
    return jax.ShapeDtypeStruct(shape, BF16)


TILES = f32_out(64, 4, 8, 128)


STRIDES = (32, 8, 2)
ALL_PARTS = tuple((part % 3, part // 3) for part in range(6))
FOUR_PARTS = ALL_PARTS[:4]
GOT_CHUNKS = 127
SEM_COUNT = 24


def axis_places(device):
    return [(device // 32) % 4, (device // 8) % 4, (device // 2) % 4], device % 2


def axis_bits(place):
    return ((place + 1) // 2) % 2, place // 2


def position(device, spec):
    places, core = axis_places(device)
    first, flip = spec
    bits = axis_bits(places[first])
    spot = (core * 2 + bits[flip]) * 2 + bits[1 - flip]
    return (spot * 4 + places[(first + 1) % 3]) * 4 + places[(first + 2) % 3]


class Exchange:
    def __init__(self, specs, buf, got, out, sends, recvs):
        self.specs, self.buf, self.got, self.out, self.sends, self.recvs = specs, buf, got, out, sends, recvs
        self.me = lax.axis_index("patch")
        self.places, self.core = axis_places(self.me)
        self.mate = self.me + 1 - 2 * self.core
        self.bits = [axis_bits(place) for place in self.places]
        self.flying = {}
        self.spot = {}
        for part, (first, flip) in enumerate(specs):
            one, two = self.bits[first][flip], self.bits[first][1 - flip]
            third, fourth = self.places[(first + 1) % 3], self.places[(first + 2) % 3]
            at_core = self.core * 64
            at_one = at_core + one * 32
            at_two = at_one + two * 16
            at_three = at_two + third * 4
            self.spot[part] = dict(
                one=one, two=two, core=at_core, first=at_one, second=at_two, third=at_three, last=at_three + fourth
            )

    def greet(self):
        mates = [self.mate]
        mates += [self.peer(axis, shift) for axis in range(3) for shift in (1, 2, 3)]
        barrier = pltpu.get_barrier_semaphore()
        for mate in mates:
            pl.semaphore_signal(barrier, inc=1, device_id=(mate,), device_id_type=MESH)
        pl.semaphore_wait(barrier, len(mates))

    def peer(self, axis, shift):
        return self.me + ((self.places[axis] + shift) % 4 - self.places[axis]) * STRIDES[axis]

    def neighbour(self, axis, flip):
        place = self.places[axis]
        step = 3 - 2 * place if flip else 1 - 2 * (place % 2)
        return self.me + step * STRIDES[axis]

    def push(self, part, sem, src, dst, device):
        copy = pltpu.make_async_remote_copy(
            src_ref=src,
            dst_ref=dst,
            send_sem=self.sends.at[sem, part],
            recv_sem=self.recvs.at[sem, part],
            device_id=(device,),
            device_id_type=MESH,
        )
        copy.start()
        self.flying[part, sem] = copy

    def wait(self, part, *sems):
        for sem in sems:
            self.flying.pop((part, sem)).wait()

    def send_sum(self, part, sem, at, size, slot, device):
        self.push(part, sem, self.buf.at[part, pl.ds(at, size)], self.got.at[part, pl.ds(slot, size)], device)

    def add(self, part, at, size, *slots):
        total = self.buf[part, pl.ds(at, size)]
        for slot in slots:
            total += self.got[part, pl.ds(slot, size)]
        self.buf[part, pl.ds(at, size)] = total

    def send_block(self, part, sem, at, size, device):
        block = self.out.at[part, pl.ds(at, size)]
        self.push(part, sem, block, block, device)


    def start(self, part):
        spot = self.spot[part]
        other = 64 - spot["core"]
        self.send_sum(part, 0, other + (1 - spot["one"]) * 32, 32, 0, self.mate)

    def start_kept(self, part):
        spot = self.spot[part]
        other = 64 - spot["core"]
        self.send_sum(part, 1, other + spot["one"] * 32, 32, 32, self.mate)

    def reduce_first(self, part):
        spot = self.spot[part]
        first, flip = self.specs[part]
        away = spot["core"] + (1 - spot["one"]) * 32
        device = self.neighbour(first, flip)
        self.wait(part, 0)
        self.add(part, away, 32, 0)
        self.send_sum(part, 2, away + (1 - spot["two"]) * 16, 16, 64, device)
        self.send_sum(part, 3, away + spot["two"] * 16, 16, 80, device)

    def reduce_kept(self, part):
        self.wait(part, 1)
        self.add(part, self.spot[part]["first"], 32, 32)

    def reduce_second(self, part):
        spot = self.spot[part]
        first, flip = self.specs[part]
        away = spot["first"] + (1 - spot["two"]) * 16
        self.wait(part, 2)
        self.add(part, away, 16, 64)
        self.send_sum(part, 4, away, 16, 96, self.neighbour(first, 1 - flip))

    def reduce_third(self, part):
        spot = self.spot[part]
        axis = (self.specs[part][0] + 1) % 3
        self.wait(part, 3, 4)
        self.add(part, spot["second"], 16, 80, 96)
        for shift in (1, 2, 3):
            at = spot["second"] + (self.places[axis] + shift) % 4 * 4
            self.send_sum(part, 4 + shift, at, 4, 108 + 4 * shift, self.peer(axis, shift))

    def reduce_fourth(self, part):
        spot = self.spot[part]
        axis = (self.specs[part][0] + 2) % 3
        self.wait(part, 5, 6, 7)
        self.add(part, spot["third"], 4, 112, 116, 120)
        for shift in (1, 2, 3):
            at = spot["third"] + (self.places[axis] + shift) % 4
            self.send_sum(part, 7 + shift, at, 1, 123 + shift, self.peer(axis, shift))

    def reduce_last(self, part):
        self.wait(part, 8, 9, 10)
        self.add(part, self.spot[part]["last"], 1, 124, 125, 126)

    def gather_fourth(self, part):
        axis = (self.specs[part][0] + 2) % 3
        for shift in (1, 2, 3):
            self.send_block(part, 10 + shift, self.spot[part]["last"], 1, self.peer(axis, shift))

    def gather_third(self, part):
        axis = (self.specs[part][0] + 1) % 3
        self.wait(part, 11, 12, 13)
        for shift in (1, 2, 3):
            self.send_block(part, 13 + shift, self.spot[part]["third"], 4, self.peer(axis, shift))

    def gather_second(self, part):
        spot = self.spot[part]
        first, flip = self.specs[part]
        self.wait(part, 14, 15, 16)
        self.send_block(part, 17, spot["second"], 16, self.neighbour(first, 1 - flip))
        self.send_block(part, 20, spot["second"], 16, self.mate)

    def gather_first(self, part):
        spot = self.spot[part]
        first, flip = self.specs[part]
        device = self.neighbour(first, flip)
        self.wait(part, 17)
        self.send_block(part, 18, spot["first"], 16, device)
        self.send_block(part, 19, spot["first"] + 16, 16, device)
        self.send_block(part, 21, spot["first"] + (1 - spot["two"]) * 16, 16, self.mate)

    def gather_core(self, part):
        spot = self.spot[part]
        self.wait(part, 18)
        self.send_block(part, 22, spot["core"] + (1 - spot["one"]) * 32, 16, self.mate)

    def gather_rest(self, part):
        spot = self.spot[part]
        self.wait(part, 19)
        self.send_block(part, 23, spot["core"] + (1 - spot["one"]) * 32 + 16, 16, self.mate)

    def gather_last(self, part):
        self.wait(part, 20, 21, 22, 23)

    REDUCE = ("reduce_first", "reduce_kept", "reduce_second", "reduce_third", "reduce_fourth", "reduce_last")
    GATHER = ("gather_fourth", "gather_third", "gather_second", "gather_first", "gather_core", "gather_rest", "gather_last")

    def run(self, stages, beside=()):
        beside = list(beside)
        for stage in stages:
            if beside:
                beside.pop(0)()
            for part in range(len(self.specs)):
                getattr(self, stage)(part)
        for work in beside:
            work()

    def finish_sum(self, part):
        self.reduce_last(part)
        last = pl.ds(self.spot[part]["last"], 1)
        self.out[part, last] = self.buf[part, last]
        self.gather_fourth(part)

    SUM = REDUCE[:-1] + ("finish_sum",) + GATHER[1:]


def exchange_scratch(parts, units):
    sem = pltpu.SemaphoreType.DMA((SEM_COUNT, parts))
    return [
        pltpu.VMEM((parts, 128, units, 8, 128), F32),
        pltpu.VMEM((parts, GOT_CHUNKS, units, 8, 128), F32),
        sem,
        sem,
    ]


def sum_out(units):
    return f32_out(LINKS, 128, units, 8, 128)


def remote_call(kernel, name_id, outs, scratch, limit, *args):
    return pl.pallas_call(
        kernel,
        out_shape=outs,
        in_specs=vmem_specs(len(args)),
        out_specs=vmem_specs(len(outs)),
        scratch_shapes=scratch,
        compiler_params=pltpu.CompilerParams(collective_id=name_id, has_side_effects=True, vmem_limit_bytes=limit << 20),
        cost_estimate=pl.CostEstimate(flops=int(3e10), bytes_accessed=int(3e7), transcendentals=0),
    )(*args)


def node_pass(feats, agg, cot, w_in, w_out):
    feat_pair, agg_pair = split(feats), split(agg)
    pre = dot3(feat_pair, pair_at(w_in, pl.ds(0, FEAT))) + dot3(agg_pair, pair_at(w_in, pl.ds(FEAT, FEAT)))
    gate = sigmoid(pre)
    hidden = split(pre * gate)
    out_pair = (w_out[0][...], w_out[1][...])
    normed, scale = norm(dot3(hidden, out_pair))
    tail = split(norm_back(cot, normed, scale))
    grad_pre = split(dot3(tail, out_pair, NT) * (gate * (1.0 + pre * (1.0 - gate))))
    return feat_pair, agg_pair, hidden, tail, grad_pre


def node_kernel(*refs):
    agg_ref, fine_ref, cot_ref, few_ref, few_cot_ref, w_in_ref, w_out_ref = refs[:7]
    grad_agg_ref, own_ref, direct_ref, node_ref = refs[7:11]
    buf, got, sends, recvs, full, wi0, wi1, wo0, wo1, total = refs[11:]
    ring = Exchange(FOUR_PARTS, buf, got, full, sends, recvs)
    ring.greet()
    for part, spec in enumerate(FOUR_PARTS):
        for device in range(128):
            first = FINE + 8 * device
            if first < NEAR and 8 * device < COARSE:
                buf[part, position(device, spec), 0] = agg_ref[first : first + 8, part * 128 : (part + 1) * 128]
            else:
                buf[part, position(device, spec), 0] = jnp.zeros((8, 128), F32)
        ring.start(part)
    for part in range(4):
        ring.start_kept(part)

    wi, wo = (wi0, wi1), (wo0, wo1)
    keep = {}

    def cut_weights():
        wi0[...], wi1[...] = split(w_in_ref[...])
        wo0[...], wo1[...] = split(w_out_ref[...])

    def fine_pass():
        keep["fine"] = node_pass(fine_ref[...], agg_ref[:FINE, :], cot_ref[...], wi, wo)

    def fine_back():
        grad_pre = keep["fine"][4]
        own_ref[...] = cot_ref[...] + dot3(grad_pre, pair_at(wi, pl.ds(0, FEAT)), NT)
        grad_agg_ref[:FINE, :] = dot3(grad_pre, pair_at(wi, pl.ds(FEAT, FEAT)), NT)

    def nothing():
        pass

    ring.run(ring.REDUCE, [nothing, cut_weights, nothing, fine_pass, fine_back])

    few_agg = jnp.concatenate([buf[part, ring.spot[part]["last"], 0] for part in range(4)], axis=1)
    blank = jnp.zeros((8, FEAT), F32)
    few = node_pass(
        jnp.concatenate([few_ref[...], blank], axis=0),
        jnp.concatenate([few_agg, blank], axis=0),
        jnp.concatenate([few_cot_ref[...], blank], axis=0),
        wi,
        wo,
    )
    few_grad = dot3(few[4], pair_at(wi, pl.ds(FEAT, FEAT)), NT)[:8]
    for part in range(4):
        full[part, ring.spot[part]["last"], 0] = few_grad[:, part * 128 : (part + 1) * 128]

    def few_back():
        direct = few_cot_ref[...] + dot3(few[4], pair_at(wi, pl.ds(0, FEAT)), NT)[:8]
        for at in range(4):
            direct_ref[at] = direct[:, at * 128 : (at + 1) * 128]

    def weights_back(which, grad, first):
        def run():
            total[...] = dot3(keep["fine"][which], keep["fine"][grad], TN) + dot3(few[which], few[grad], TN)
            put_tiles(node_ref.at[pl.ds(first, 64)], total)

        return run

    beside = [nothing, few_back, weights_back(0, 4, 0), weights_back(1, 4, 64), weights_back(2, 3, 128)]
    ring.run(ring.GATHER, beside)
    for part, spec in enumerate(FOUR_PARTS):
        for device in range((NEAR - FINE) // 8):
            first = FINE + 8 * device
            grad_agg_ref[first : first + 8, part * 128 : (part + 1) * 128] = full[part, position(device, spec), 0]


def node_step(agg, fine, cot_fine, few, few_cot, w_in, w_out):
    half = pltpu.VMEM((2 * FEAT, FEAT), BF16)
    quarter = pltpu.VMEM((FEAT, FEAT), BF16)
    return remote_call(
        node_kernel,
        2,
        [f32_out(NEAR, FEAT), f32_out(FINE, FEAT), f32_out(4, 8, 128), f32_out(192, 4, 8, 128)],
        exchange_scratch(4, 1)
        + [pltpu.VMEM((4, 128, 1, 8, 128), F32), half, half, quarter, quarter, pltpu.VMEM((FEAT, FEAT), F32)],
        34,
        agg,
        fine,
        cot_fine,
        few,
        few_cot,
        w_in,
        w_out,
    )


CHIPS = 64


class Shuffle:
    def __init__(self, sends, recvs, core_sends, core_recvs):
        self.sends, self.recvs, self.core_sends, self.core_recvs = sends, recvs, core_sends, core_recvs
        self.me = lax.axis_index("patch")
        self.places, self.core = axis_places(self.me)
        self.chip = self.me // 2
        self.mate = self.me + 1 - 2 * self.core

    def other(self, step):
        z, x, y = ((place + step // span) % 4 for place, span in zip(self.places, (16, 4, 1)))
        return z * 16 + x * 4 + y

    def each(self, run):
        def body(step, carry):
            run(self.other(step))
            return carry

        lax.fori_loop(1, CHIPS, body, 0)

    def signal(self):
        barrier = pltpu.get_barrier_semaphore()

        def run(chip):
            pl.semaphore_signal(barrier, inc=1, device_id=(chip * 2 + self.core,), device_id_type=MESH)

        self.each(run)
        pl.semaphore_signal(barrier, inc=1, device_id=(self.mate,), device_id_type=MESH)

    def wait_signals(self):
        pl.semaphore_wait(pltpu.get_barrier_semaphore(), CHIPS)

    def copy(self, src, dst, sends, recvs, device):
        return pltpu.make_async_remote_copy(
            src_ref=src, dst_ref=dst, send_sem=sends, recv_sem=recvs, device_id=(device,), device_id_type=MESH
        )

    def send_chips(self, src, dst):
        def run(chip):
            self.copy(src.at[chip], dst.at[self.chip], self.sends, self.recvs, chip * 2 + self.core).start()

        self.each(run)
        dst[self.chip] = src[self.chip]

    def wait_chips(self, src, dst):
        most = pl.ds(0, CHIPS - 1)
        self.copy(src.at[most], dst.at[most], self.sends, self.recvs, self.mate).wait()

    def core_copy(self, src, dst):
        return self.copy(src, dst, self.core_sends, self.core_recvs, self.mate)


def front_kernel(*refs):
    fine_ref, near_ref, edge_ref, w_ref, w_out_ref, list_ref, send_ref, recv_ref = refs[:8]
    pre_ref, normed_ref, scale_ref, agg_ref = refs[8:12]
    outgoing, got, from_mate, p0, p1, q0, q1, h0, h1, n0, n1, rep, recv_rep = refs[12:25]
    shuffle = Shuffle(*refs[25:])
    shuffle.signal()
    w_send = split(w_ref[FEAT : 2 * FEAT, :])
    own = split(dot3(split(fine_ref[...]), w_send))
    p0[pl.ds(0, FINE), :], p1[pl.ds(0, FINE), :] = own
    rep[...] = spread(list_ref[...])

    def request(at, carry):
        rows = block_at(at)
        chips = pl.ds(at * (BLOCK // 16), BLOCK // 16)
        outgoing[chips] = dot2(hot_rows(rep[rows, :], 0, FINE), own).reshape(BLOCK // 16, 2, 8, FEAT)
        return carry

    lax.fori_loop(0, EDGE // BLOCK, request, 0)
    shuffle.wait_signals()
    shuffle.send_chips(outgoing, got)

    rep[...] = spread(send_ref[...])
    recv_rep[...] = spread(recv_ref[...])
    w_recv = split(w_ref[2 * FEAT :, :])
    put_pair((q0, q1), pl.ds(0, FINE), dot3(split(near_ref[:FINE, :]), w_recv))

    def project(at, carry):
        rows = block_at(at)
        feats = split(near_ref[rows, :])
        put_pair((p0, p1), rows, dot3(feats, w_send))
        put_pair((q0, q1), rows, dot3(feats, w_recv))
        return carry

    lax.fori_loop(1, NEAR // BLOCK, project, 0)
    w_edge = split(w_ref[:FEAT, :])

    def near_step(at, carry):
        rows = block_at(at)
        total = dot3(split(edge_ref[rows, :]), w_edge)
        total += dot2(hot_rows(recv_rep[rows, :], 0, NEAR), (q0[...], q1[...]))
        total += dot2(hot_rows(rep[rows, :], 0, NEAR), (p0[...], p1[...]))
        pre_ref[rows, :] = total
        return carry

    lax.fori_loop(0, EDGE // BLOCK, near_step, 0)

    shuffle.wait_chips(outgoing, got)
    swap = shuffle.core_copy(got.at[:, 1 - shuffle.core], from_mate)
    swap.start()
    half = CHIPS * 8
    put_pair((h0, h1), pl.ds(0, half), got[:, shuffle.core].reshape(half, FEAT))
    w_out = split(w_out_ref[...])
    swap.wait()
    put_pair((h0, h1), pl.ds(half, half), from_mate[...].reshape(half, FEAT))

    def edge_step(at, carry):
        rows = block_at(at)
        pre = pre_ref[rows, :] + dot2(hot_rows(rep[rows, :], NEAR, EDGE), (h0[...], h1[...]))
        pre_ref[rows, :] = pre
        normed, scale = norm(dot3(split(pre * sigmoid(pre)), w_out))
        normed_ref[rows, :] = normed
        scale_ref[rows, :] = jnp.broadcast_to(scale, (BLOCK, 128))
        put_pair((n0, n1), rows, edge_ref[rows, :] + normed)
        return carry

    lax.fori_loop(0, EDGE // BLOCK, edge_step, 0)

    def gather(at, carry):
        rows = block_at(at)
        agg_ref[rows, :] = dot2(hot_columns(recv_ref[...], at * BLOCK, BLOCK), (n0[...], n1[...]))
        return carry

    lax.fori_loop(0, NEAR // BLOCK, gather, 0)


def back_kernel(*refs):
    grad_agg_ref, cot_ref, pre_ref, normed_ref, scale_ref, w_out_ref, send_ref, recv_ref = refs[:8]
    edge_ref, near_ref, w_ref, list_ref, direct_ref = refs[8:13]
    grad_edges_ref, grad_fine_ref, in_edge_ref, out_ref, in_recv_ref, coarse_ref, in_send_ref = refs[13:20]
    t0, t1, d0, d1, a0, a1, recv_rep, for_mate, pack, back = refs[20:30]
    edge_total, tail_total, recv_total, send_total = refs[30:34]
    shuffle = Shuffle(*refs[34:])
    shuffle.signal()
    recv_rep[...] = spread(recv_ref[...])
    a0[...], a1[...] = split(grad_agg_ref[...])
    w_out = split(w_out_ref[...])

    def step(at, carry):
        rows = block_at(at)
        grad = cot_ref[rows, :] + dot2(hot_rows(recv_rep[rows, :], 0, NEAR), (a0[...], a1[...]))
        grad_edges_ref[rows, :] = grad
        tail = split(norm_back(grad, normed_ref[rows, :], scale_ref[rows, :1]))
        t0[rows, :], t1[rows, :] = tail
        pre = pre_ref[rows, :]
        gate = sigmoid(pre)
        put_pair((d0, d1), rows, dot3(tail, w_out, NT) * (gate * (1.0 + pre * (1.0 - gate))))
        return carry

    lax.fori_loop(0, EDGE // BLOCK, step, 0)

    def halo_rows(first, at):
        rows = dot2(hot_columns(send_ref[...], NEAR + first + at * BLOCK, BLOCK), (d0[...], d1[...]))
        return rows.reshape(BLOCK // 8, 8, FEAT)

    half = CHIPS * 8

    def to_mate(at, carry):
        for_mate[pl.ds(at * (BLOCK // 8), BLOCK // 8)] = halo_rows(half, at)
        return carry

    def to_pack(at, carry):
        pack[pl.ds(at * (BLOCK // 8), BLOCK // 8), 0] = halo_rows(0, at)
        return carry

    lax.fori_loop(0, half // BLOCK, to_mate, 0)
    shuffle.wait_signals()
    swap = shuffle.core_copy(for_mate, pack.at[:, 1])
    swap.start()
    lax.fori_loop(0, half // BLOCK, to_pack, 0)
    swap.wait()
    shuffle.send_chips(pack, back)

    edge_total[...] = jnp.zeros_like(edge_total)
    tail_total[...] = jnp.zeros_like(tail_total)
    w_edge = split(w_ref[:FEAT, :])

    def weight_step(at, carry):
        rows = block_at(at)
        grad_pre = (d0[rows, :], d1[rows, :])
        grad_edges_ref[rows, :] += dot3(grad_pre, w_edge, NT)
        edge_total[...] += dot3(split(edge_ref[rows, :]), grad_pre, TN)
        pre = pre_ref[rows, :]
        tail_total[...] += dot3(split(pre * sigmoid(pre)), (t0[rows, :], t1[rows, :]), TN)
        return carry

    lax.fori_loop(0, EDGE // BLOCK, weight_step, 0)
    put_tiles(in_edge_ref, edge_total)
    put_tiles(out_ref, tail_total)
    w_send = split(w_ref[FEAT : 2 * FEAT, :])
    w_recv = split(w_ref[2 * FEAT :, :])

    def sums(at):
        grad_pre = (d0[...], d1[...])
        sent = dot2(hot_columns(send_ref[...], at * BLOCK, BLOCK), grad_pre)
        return sent, split(dot2(hot_columns(recv_ref[...], at * BLOCK, BLOCK), grad_pre))

    fine_sent, received = sums(0)
    grad_fine_ref[...] = direct_ref[...] + dot3(received, w_recv, NT)
    recv_total[...] = dot3(split(near_ref[:FINE, :]), received, TN)
    send_total[...] = jnp.zeros_like(send_total)

    def coarse_step(at, carry):
        rows = block_at(at)
        sent, received = sums(at)
        sent = split(sent)
        value = dot3(sent, w_send, NT) + dot3(received, w_recv, NT)
        put_tiles(coarse_ref.at[pl.ds((at - 1) * (BLOCK // 8), BLOCK // 8)], value)
        feats = split(near_ref[rows, :])
        recv_total[...] += dot3(feats, received, TN)
        send_total[...] += dot3(feats, sent, TN)
        return carry

    lax.fori_loop(1, NEAR // BLOCK, coarse_step, 0)
    put_tiles(in_recv_ref, recv_total)

    shuffle.wait_chips(pack, back)
    returned = split(back[...].reshape(EDGE, FEAT))
    fine_sent = split(fine_sent + dot2(hot_columns(list_ref[...], 0, FINE), returned))
    grad_fine_ref[...] += dot3(fine_sent, w_send, NT)
    send_total[...] += dot3(split(near_ref[:FINE, :]), fine_sent, TN)
    put_tiles(in_send_ref, send_total)


OUT_ROW, EDGE_ROW, RECV_ROW, COARSE_ROW, SEND_ROW, ROWS = 192, 256, 320, 384, 480, 576


def sum_kernel(*refs):
    node_ref, out_ref, in_edge_ref, in_recv_ref, coarse_ref, in_send_ref, direct_ref = refs[:7]
    sum_ref, buf, got, sends, recvs = refs[7:]
    flat = buf.reshape(ROWS * 4, 8, 128)
    ring = Exchange(ALL_PARTS, buf, got, sum_ref, sends, recvs)
    ring.greet()
    started = 0
    row = 0
    for ref in (node_ref, out_ref, in_edge_ref, in_recv_ref, coarse_ref, in_send_ref):
        size = ref.shape[0]
        flat[row * 4 : (row + size) * 4] = ref[...].reshape(size * 4, 8, 128)
        if row == COARSE_ROW:
            flat[pl.ds(row * 4 + ring.me % 96 * 4, 4)] += direct_ref[...]
        row += size
        if row == SEND_ROW + 64:
            flat[row * 4 :] = jnp.zeros(((ROWS - row) * 4, 8, 128), F32)
            row = ROWS
        while started < LINKS and (started + 1) * (ROWS // LINKS) <= row:
            ring.start(started)
            started += 1
    for part in range(LINKS):
        ring.start_kept(part)
    ring.run(ring.SUM)


def put_rows(ref, tiles, scale):
    for at in range(FEAT // 128):
        ref[:, at * 128 : (at + 1) * 128] = (tiles[:, at] * scale).reshape(-1, 128)


def finish_kernel(edge_scale, node_scale, sum_ref, coarse_ref, in_ref, out_ref, node_in_ref, node_out_ref):
    tiles = sum_ref.reshape(ROWS, 4, 8, 128)
    for place, row in enumerate((EDGE_ROW, SEND_ROW, RECV_ROW)):
        put_rows(in_ref.at[pl.ds(place * FEAT, FEAT)], tiles[row : row + 64], edge_scale)
    put_rows(out_ref, tiles[OUT_ROW : OUT_ROW + 64], edge_scale)
    whole = COARSE // 8
    put_rows(coarse_ref.at[pl.ds(0, whole * 8)], tiles[COARSE_ROW : COARSE_ROW + whole], 1.0)
    for at in range(FEAT // 128):
        coarse_ref[whole * 8 :, at * 128 : (at + 1) * 128] = tiles[COARSE_ROW + whole, at][: COARSE - whole * 8]
    put_rows(node_in_ref, tiles[0:128], node_scale)
    put_rows(node_out_ref, tiles[128:192], node_scale)


def per_device(
    fine_nodes,
    coarse_nodes,
    edge_feats,
    senders,
    receivers,
    send_rows,
    w_edge_in,
    w_edge_out,
    w_node_in,
    w_node_out,
    cot_fine,
    cot_coarse,
    cot_edges,
):
    me = lax.axis_index("patch")
    peers = lax.axis_size("patch")
    core = me % 2
    near_count = FINE + COARSE
    send_list = send_rows.reshape(CHIPS, 2, 8)
    back_list = jnp.where(core == 1, send_list[:, ::-1], send_list).reshape(1, EDGE)
    send_list = send_list.reshape(1, EDGE)
    halo = senders - near_count
    source = halo // 8
    halo_at = NEAR + (source % 2 != core) * (EDGE // 2) + source // 2 * 8 + halo % 8
    send_at = jnp.where(senders < near_count, senders, halo_at).astype(jnp.int32).reshape(1, EDGE)
    recv_at = receivers.reshape(1, EDGE)
    half = pltpu.VMEM((EDGE, FEAT), BF16)
    index = pltpu.VMEM((EDGE, 128), jnp.int32)
    square = pltpu.VMEM((FEAT, FEAT), F32)
    chip_rows = pltpu.VMEM((CHIPS, 2, 8, FEAT), F32)
    core_rows = pltpu.VMEM((CHIPS, 8, FEAT), F32)
    sems = [pltpu.SemaphoreType.DMA] * 4
    wide = f32_out(EDGE, FEAT)
    fine_out = f32_out(FINE, FEAT)

    near = jnp.concatenate([fine_nodes, coarse_nodes, jnp.zeros((NEAR - near_count, FEAT), F32)], axis=0)
    pre, normed, scale, agg = remote_call(
        front_kernel,
        1,
        [wide, wide, f32_out(EDGE, 128), wide],
        [chip_rows, chip_rows, core_rows] + [half] * 8 + [index] * 2 + sems,
        FRONT_MIB,
        fine_nodes,
        near,
        edge_feats,
        w_edge_in,
        w_edge_out,
        send_list,
        send_at,
        recv_at,
    )
    blank = jnp.zeros((8 * peers - COARSE, FEAT), F32)
    few = lax.dynamic_slice(jnp.concatenate([coarse_nodes, blank], axis=0), (me * 8, 0), (8, FEAT))
    few_cot = lax.dynamic_slice(jnp.concatenate([cot_coarse, blank], axis=0), (me * 8, 0), (8, FEAT))
    grad_agg, direct, few_direct, node = node_step(agg, fine_nodes, cot_fine, few, few_cot, w_node_in, w_node_out)
    grad_edges, grad_fine, in_edge, edge_out, in_recv, coarse, in_send = remote_call(
        back_kernel,
        3,
        [wide, fine_out, TILES, TILES, TILES, f32_out(96, 4, 8, 128), TILES],
        [half] * 6 + [index, core_rows, chip_rows, chip_rows] + [square] * 4 + sems,
        BACK_MIB,
        grad_agg,
        cot_edges,
        pre,
        normed,
        scale,
        w_edge_out,
        send_at,
        recv_at,
        edge_feats,
        near,
        w_edge_in,
        back_list,
        direct,
    )
    (summed,) = remote_call(
        sum_kernel, 4, [sum_out(3)], exchange_scratch(LINKS, 3), SUM_MIB, node, edge_out, in_edge, in_recv, coarse, in_send, few_direct
    )
    grad_coarse, grad_in, grad_out, grad_node_in, grad_node_out = local_call(
        functools.partial(
            finish_kernel, 1.0 / math.sqrt(EDGE * peers), 1.0 / math.sqrt(FINE * peers + COARSE)
        ),
        [f32_out(COARSE, FEAT), f32_out(3 * FEAT, FEAT), f32_out(FEAT, FEAT), f32_out(2 * FEAT, FEAT), f32_out(FEAT, FEAT)],
        [],
        1e6,
        summed,
    )
    return grad_fine, grad_coarse, grad_edges, grad_in, grad_out, grad_node_in, grad_node_out


def solution(mesh):
    return jax.shard_map(
        per_device,
        mesh=mesh,
        in_specs=(
            P("patch", None),
            P(),
            P("patch", None),
            P("patch"),
            P("patch"),
            P("patch", None, None),
            P(),
            P(),
            P(),
            P(),
            P("patch", None),
            P(),
            P("patch", None),
        ),
        out_specs=(P("patch", None), P(), P("patch", None), P(), P(), P(), P()),
        check_vma=False,
    )
```

profile of v0, /device:TPU:1, one launch (start us, length us, event | category | flops | bytes accessed | tf_op | source)
XLA Modules:
  0.0 231.0 jit_solution(14325922562891027570)
XLA Ops:
  0.6 0.0 copy-start.2
  0.6 0.0 copy-start.12
  0.7 0.1 pad.4.clone
  0.8 0.7 compare_select_fusion
  1.5 0.0 copy-start.5
  1.5 0.9 pad_dynamic-slice_fusion
  2.4 0.0 copy-done.12
  2.4 0.1 copy.23
  2.5 0.1 reshape_reshape.3.refs_5_
  2.6 0.1 rev.3
  2.7 0.0 copy-start.9
  2.8 0.1 reshape.29.refs_11_
  2.9 0.0 copy-done.2
  2.9 0.0 copy-start.3
  2.9 1.7 maximum_maximum_fusion.refs_1_.refs_9_
  4.6 0.0 copy-done.5
  4.6 0.0 copy-done.9
  4.6 0.6 copy-done.3
  5.3 0.0 copy-start.7
  5.3 1.2 copy-done.7
  6.5 0.0 copy-start.1
  6.5 0.0 copy-start.4
  6.5 0.0 copy-start.6
  6.5 0.0 copy-start.8
  6.5 55.4 %shard_map.180 = (f32[1024,512]{1,0:T(8,128)S(1)}, f32[1024,512]{1,0:T(8,128)S(1)}, f32[1024,128]{1,0:T(8,128)S(1)}, f32[1024,512]{1,0:T(8,128)S(1)}) custom-call(f32[256,512]{1,0:T(8,128)S(1)} %copy-done.2, f32[1024,512]{1,0:T(8,128)S(1)} %maximum_maximum_fusion.refs_1_.refs_9_, f32[1024,512]{1,0:T(8,128)S(1)} %copy-done.5, f32[1536,512]{1,0:T(8,128)S(1)} %copy-done.3, ...), custom_call_target="tpu_custom_call" | custom-call | flops 30000001024 | bytes 30000000 | tf_op jit(solution)/shard_map/pallas_call | solution.py:347
  61.9 0.0 copy-done.1
  61.9 0.0 copy-start.10
  61.9 1.3 copy-done.10
  63.2 0.0 copy-start.11
  63.2 0.0 copy-done.4
  63.2 0.0 copy-done.6
  63.2 0.0 copy-done.8
  63.2 41.6 %shard_map.181 = (f32[1024,512]{1,0:T(8,128)S(1)}, f32[256,512]{1,0:T(8,128)S(1)}, f32[4,8,128]{2,1,0:T(8,128)S(1)}, f32[192,4,8,128]{3,2,1,0:T(8,128)S(1)}) custom-call(f32[1024,512]{1,0:T(8,128)S(1)} %get-tuple-element.27.refs_0_, f32[256,512]{1,0:T(8,128)S(1)} %copy-done.2, f32[256,512]{1,0:T(8,128)S(1)} %copy-done.8, ...), custom_call_target="tpu_custom_call" | custom-call | flops 30000001024 | bytes 30000000 | tf_op jit(solution)/shard_map/pallas_call | solution.py:347
  104.8 0.0 copy-done.11
  104.8 50.9 %shard_map.182 = (f32[1024,512]{1,0:T(8,128)S(1)}, f32[256,512]{1,0:T(8,128)S(1)}, f32[64,4,8,128]{3,2,1,0:T(8,128)S(1)}, f32[64,4,8,128]{3,2,1,0:T(8,128)S(1)},...) custom-call(f32[1024,512]{1,0:T(8,128)S(1)} %get-tuple-element.28.refs_0_, ...), custom_call_target="tpu_custom_call" | custom-call | flops 30000001024 | bytes 30000000 | tf_op jit(solution)/shard_map/pallas_call | solution.py:347
  155.8 65.2 %shard_map.183.sum_ref = f32[6,128,3,8,128]{4,3,2,1,0:T(8,128)} custom-call(f32[192,4,8,128]{3,2,1,0:T(8,128)S(1)} %get-tuple-element.34.refs_0_, f32[64,4,8,128]{3,2,1,0:T(8,128)S(1)} %get-tuple-element.35.refs_1_, f32[64,4,8,128]{3,2,1,0:T(8,128)S(1)} %get-tuple-element.36.refs_2_, f32[64,4,8,128]{3,2,1,0:T(8,128)S(1)} %get-tuple-element.37.refs_3_, ...), custom_call_target="tpu_custom_call" | custom-call | flops 30000001024 | bytes 30000000 | tf_op jit(solution)/shard_map/pallas_call | solution.py:347
  221.0 0.0 copy-start
  221.0 3.7 %copy-done = f32[6,128,3,8,128]{4,3,2,1,0:T(8,128)S(1)} copy-done((f32[6,128,3,8,128]{4,3,2,1,0:T(8,128)S(1)}, f32[6,128,3,8,128]{4,3,2,1,0:T(8,128)}, u32[]{:S(2)}) %copy-start) | copy-done | bytes 9437208
  224.6 4.3 %shard_map.184 = (f32[642,512]{1,0:T(8,128)}, f32[1536,512]{1,0:T(8,128)}, f32[512,512]{1,0:T(8,128)}, f32[1024,512]{1,0:T(8,128)}, f32[512,512]{1,0:T(8,128)}) custom-call(f32[6,128,3,8,128]{4,3,2,1,0:T(8,128)S(1)} %copy-done), custom_call_target="tpu_custom_call" | custom-call | flops 1000000 | bytes 18092032 | tf_op jit(solution)/shard_map/pallas_call | solution.py:105
  228.9 0.8 copy.27
  229.7 1.3 copy.28
  (2 shorter events, 0.0 us)
Async XLA Ops:
  0.6 2.3 copy-start.2
  0.6 1.7 copy-start.12
  1.5 3.1 %copy-start.5 = (f32[1024,512]{1,0:T(8,128)S(1)}, f32[1024,512]{1,0:T(8,128)}, u32[]{:S(2)}) copy-start(f32[1024,512]{1,0:T(8,128)} %refs_8_.1) | copy-start | bytes 6291460
  2.7 1.9 copy-start.9
  2.9 2.4 %copy-start.3 = (f32[1536,512]{1,0:T(8,128)S(1)}, f32[1536,512]{1,0:T(8,128)}, u32[]{:S(2)}) copy-start(f32[1536,512]{1,0:T(8,128)} %refs_10_.1) | copy-start | bytes 9437188
  5.3 1.2 copy-start.7
  6.5 55.4 %copy-start.1 = (f32[1024,512]{1,0:T(8,128)}, f32[1024,512]{1,0:T(8,128)S(1)}, u32[]{:S(2)}) copy-start(f32[1024,512]{1,0:T(8,128)S(1)} %maximum_maximum_fusion.refs_1_.refs_9_) | copy-start | bytes 6291460
  6.5 56.8 %copy-start.4 = (f32[1024,512]{1,0:T(8,128)S(1)}, f32[1024,512]{1,0:T(8,128)}, u32[]{:S(2)}) copy-start(f32[1024,512]{1,0:T(8,128)} %refs_5_.2) | copy-start | bytes 6291460
  6.5 56.8 %copy-start.6 = (f32[512,512]{1,0:T(8,128)S(1)}, f32[512,512]{1,0:T(8,128)}, u32[]{:S(2)}) copy-start(f32[512,512]{1,0:T(8,128)} %refs_6_.1) | copy-start | bytes 3145732
  6.5 56.8 %copy-start.8 = (f32[256,512]{1,0:T(8,128)S(1)}, f32[256,512]{1,0:T(8,128)}, u32[]{:S(2)}) copy-start(f32[256,512]{1,0:T(8,128)} %refs_2_.3) | copy-start | bytes 1572868
  61.9 1.3 copy-start.10
  63.2 41.6 %copy-start.11 = (f32[1024,512]{1,0:T(8,128)}, f32[1024,512]{1,0:T(8,128)S(1)}, u32[]{:S(2)}) copy-start(f32[1024,512]{1,0:T(8,128)S(1)} %get-tuple-element.30.refs_3_) | copy-start | bytes 6291460
  221.0 3.7 %copy-start = (f32[6,128,3,8,128]{4,3,2,1,0:T(8,128)S(1)}, f32[6,128,3,8,128]{4,3,2,1,0:T(8,128)}, u32[]{:S(2)}) copy-start(f32[6,128,3,8,128]{4,3,2,1,0:T(8,128)} %shard_map.183.sum_ref) | copy-start | bytes 28311556
where the time goes:
time: 231 us
  Pallas kernels  217 us (94%)
  local copies, waits for them, and re-layouts  10.5 us (5%)
  other arithmetic  2.4 us (1%)
    pallas_call x4, Pallas kernels, remote_call(): pl.pallas_call(kernel, out_shape=outs, in_specs=vmem_specs(len(args)), ou...  213 us
    unnamed x29, local copies, waits for them, and re-layouts  9.11 us

commit v1 on v0

--- a/solution.py
+++ b/solution.py
@@ -18,8 +18,8 @@
 EDGE = 1024
 BLOCK = 256
 LINKS = 6
-LOCAL_BYTES = 30 << 20
-FRONT_MIB, BACK_MIB, SUM_MIB = 36, 40, 40
+WIDE = 512
+FRONT_MIB, BACK_MIB, SUM_MIB = 38, 42, 30
 
 NN = (((1,), (0,)), ((), ()))
 NT = (((1,), (1,)), ((), ()))
@@ -43,8 +43,8 @@
     return dot(left, right[0], dims) + dot(left, right[1], dims)
 
 
-def block_at(step):
-    return pl.ds(pl.multiple_of(step * BLOCK, BLOCK), BLOCK)
+def block_at(step, size=BLOCK):
+    return pl.ds(pl.multiple_of(step * size, size), size)
 
 
 def pair_at(refs, rows):
@@ -98,19 +98,6 @@
 
 def vmem_specs(count):
     return [pl.BlockSpec(memory_space=pltpu.VMEM)] * count
-
-
-def local_call(kernel, outs, scratch, flops, *args):
-    moved = sum(math.prod(a.shape) * 4 for a in args) + sum(math.prod(o.shape) * 4 for o in outs)
-    return pl.pallas_call(
-        kernel,
-        out_shape=outs,
-        in_specs=vmem_specs(len(args)),
-        out_specs=vmem_specs(len(outs)),
-        scratch_shapes=scratch,
-        compiler_params=pltpu.CompilerParams(vmem_limit_bytes=LOCAL_BYTES),
-        cost_estimate=pl.CostEstimate(flops=int(flops), bytes_accessed=moved, transcendentals=0),
-    )(*args)
 
 
 def f32_out(*shape):
@@ -355,16 +342,33 @@
     )(*args)
 
 
-def node_pass(feats, agg, cot, w_in, w_out):
-    feat_pair, agg_pair = split(feats), split(agg)
-    pre = dot3(feat_pair, pair_at(w_in, pl.ds(0, FEAT))) + dot3(agg_pair, pair_at(w_in, pl.ds(FEAT, FEAT)))
-    gate = sigmoid(pre)
-    hidden = split(pre * gate)
-    out_pair = (w_out[0][...], w_out[1][...])
-    normed, scale = norm(dot3(hidden, out_pair))
-    tail = split(norm_back(cot, normed, scale))
-    grad_pre = split(dot3(tail, out_pair, NT) * (gate * (1.0 + pre * (1.0 - gate))))
-    return feat_pair, agg_pair, hidden, tail, grad_pre
+def few_dot3(left, right, dims=NN):
+    count = left[0].shape[0]
+    both = dot(jnp.concatenate(left, axis=0), right[0], dims)
+    return both[:count] + both[count:] + dot(left[0], right[1], dims)
+
+
+class NodePass:
+    def __init__(self, product, w_in, w_out):
+        self.product, self.w_in, self.w_out = product, w_in, w_out
+
+    def first(self, feats, agg):
+        self.feats, self.agg = split(feats), split(agg)
+        pre = self.product(self.feats, pair_at(self.w_in, pl.ds(0, FEAT)))
+        self.pre = pre + self.product(self.agg, pair_at(self.w_in, pl.ds(FEAT, FEAT)))
+        self.gate = sigmoid(self.pre)
+        self.hidden = split(self.pre * self.gate)
+
+    def second(self):
+        self.normed, self.scale = norm(self.product(self.hidden, pair_at(self.w_out, pl.ds(0, FEAT))))
+
+    def third(self, cot):
+        self.tail = split(norm_back(cot, self.normed, self.scale))
+        grad = self.product(self.tail, pair_at(self.w_out, pl.ds(0, FEAT)), NT)
+        self.grad = split(grad * (self.gate * (1.0 + self.pre * (1.0 - self.gate))))
+
+    def back(self, first):
+        return self.product(self.grad, pair_at(self.w_in, pl.ds(first, FEAT)), NT)
 
 
 def node_kernel(*refs):
@@ -385,51 +389,53 @@
         ring.start_kept(part)
 
     wi, wo = (wi0, wi1), (wo0, wo1)
-    keep = {}
+    fine = NodePass(dot3, wi, wo)
+    few = NodePass(few_dot3, wi, wo)
 
     def cut_weights():
         wi0[...], wi1[...] = split(w_in_ref[...])
         wo0[...], wo1[...] = split(w_out_ref[...])
 
-    def fine_pass():
-        keep["fine"] = node_pass(fine_ref[...], agg_ref[:FINE, :], cot_ref[...], wi, wo)
+    def fine_first():
+        fine.first(fine_ref[...], agg_ref[:FINE, :])
+
+    def fine_third():
+        fine.third(cot_ref[...])
 
     def fine_back():
-        grad_pre = keep["fine"][4]
-        own_ref[...] = cot_ref[...] + dot3(grad_pre, pair_at(wi, pl.ds(0, FEAT)), NT)
-        grad_agg_ref[:FINE, :] = dot3(grad_pre, pair_at(wi, pl.ds(FEAT, FEAT)), NT)
+        own_ref[...] = cot_ref[...] + fine.back(0)
+
+    def fine_agg():
+        grad_agg_ref[:FINE, :] = fine.back(FEAT)
+
+    ring.run(ring.REDUCE, [cut_weights, fine_first, fine.second, fine_third, fine_back, fine_agg])
+
+    few_agg = jnp.concatenate([buf[part, ring.spot[part]["last"], 0] for part in range(4)], axis=1)
+    blank = jnp.zeros((8, FEAT), F32)
+    few.first(jnp.concatenate([few_ref[...], blank], axis=0), jnp.concatenate([few_agg, blank], axis=0))
+    few.second()
+    few.third(jnp.concatenate([few_cot_ref[...], blank], axis=0))
+    few_grad = few.back(FEAT)[:8]
+    for part in range(4):
+        full[part, ring.spot[part]["last"], 0] = few_grad[:, part * 128 : (part + 1) * 128]
+
+    def few_back():
+        direct = few_cot_ref[...] + few.back(0)[:8]
+        for at in range(4):
+            direct_ref[at] = direct[:, at * 128 : (at + 1) * 128]
+
+    def weights_back(which, grad, first):
+        def run():
+            total[...] = dot3(getattr(fine, which), getattr(fine, grad), TN) + dot3(getattr(few, which), getattr(few, grad), TN)
+            put_tiles(node_ref.at[pl.ds(first, 64)], total)
+
+        return run
 
     def nothing():
         pass
 
-    ring.run(ring.REDUCE, [nothing, cut_weights, nothing, fine_pass, fine_back])
-
-    few_agg = jnp.concatenate([buf[part, ring.spot[part]["last"], 0] for part in range(4)], axis=1)
-    blank = jnp.zeros((8, FEAT), F32)
-    few = node_pass(
-        jnp.concatenate([few_ref[...], blank], axis=0),
-        jnp.concatenate([few_agg, blank], axis=0),
-        jnp.concatenate([few_cot_ref[...], blank], axis=0),
-        wi,
-        wo,
-    )
-    few_grad = dot3(few[4], pair_at(wi, pl.ds(FEAT, FEAT)), NT)[:8]
-    for part in range(4):
-        full[part, ring.spot[part]["last"], 0] = few_grad[:, part * 128 : (part + 1) * 128]
-
-    def few_back():
-        direct = few_cot_ref[...] + dot3(few[4], pair_at(wi, pl.ds(0, FEAT)), NT)[:8]
-        for at in range(4):
-            direct_ref[at] = direct[:, at * 128 : (at + 1) * 128]
-
-    def weights_back(which, grad, first):
-        def run():
-            total[...] = dot3(keep["fine"][which], keep["fine"][grad], TN) + dot3(few[which], few[grad], TN)
-            put_tiles(node_ref.at[pl.ds(first, 64)], total)
-
-        return run
-
-    beside = [nothing, few_back, weights_back(0, 4, 0), weights_back(1, 4, 64), weights_back(2, 3, 128)]
+    beside = [nothing, few_back]
+    beside += [weights_back("feats", "grad", 0), weights_back("agg", "grad", 64), weights_back("hidden", "tail", 128)]
     ring.run(ring.GATHER, beside)
     for part, spec in enumerate(FOUR_PARTS):
         for device in range((NEAR - FINE) // 8):
@@ -519,43 +525,41 @@
     shuffle.signal()
     w_send = split(w_ref[FEAT : 2 * FEAT, :])
     own = split(dot3(split(fine_ref[...]), w_send))
-    p0[pl.ds(0, FINE), :], p1[pl.ds(0, FINE), :] = own
     rep[...] = spread(list_ref[...])
 
     def request(at, carry):
-        rows = block_at(at)
-        chips = pl.ds(at * (BLOCK // 16), BLOCK // 16)
-        outgoing[chips] = dot2(hot_rows(rep[rows, :], 0, FINE), own).reshape(BLOCK // 16, 2, 8, FEAT)
+        rows = block_at(at, WIDE)
+        chips = pl.ds(at * (WIDE // 16), WIDE // 16)
+        outgoing[chips] = dot2(hot_rows(rep[rows, :], 0, FINE), own).reshape(WIDE // 16, 2, 8, FEAT)
         return carry
 
-    lax.fori_loop(0, EDGE // BLOCK, request, 0)
+    lax.fori_loop(0, EDGE // WIDE, request, 0)
     shuffle.wait_signals()
     shuffle.send_chips(outgoing, got)
 
     rep[...] = spread(send_ref[...])
     recv_rep[...] = spread(recv_ref[...])
     w_recv = split(w_ref[2 * FEAT :, :])
-    put_pair((q0, q1), pl.ds(0, FINE), dot3(split(near_ref[:FINE, :]), w_recv))
 
     def project(at, carry):
-        rows = block_at(at)
+        rows = block_at(at, WIDE)
         feats = split(near_ref[rows, :])
         put_pair((p0, p1), rows, dot3(feats, w_send))
         put_pair((q0, q1), rows, dot3(feats, w_recv))
         return carry
 
-    lax.fori_loop(1, NEAR // BLOCK, project, 0)
+    lax.fori_loop(0, NEAR // WIDE, project, 0)
     w_edge = split(w_ref[:FEAT, :])
 
     def near_step(at, carry):
-        rows = block_at(at)
+        rows = block_at(at, WIDE)
         total = dot3(split(edge_ref[rows, :]), w_edge)
         total += dot2(hot_rows(recv_rep[rows, :], 0, NEAR), (q0[...], q1[...]))
         total += dot2(hot_rows(rep[rows, :], 0, NEAR), (p0[...], p1[...]))
         pre_ref[rows, :] = total
         return carry
 
-    lax.fori_loop(0, EDGE // BLOCK, near_step, 0)
+    lax.fori_loop(0, EDGE // WIDE, near_step, 0)
 
     shuffle.wait_chips(outgoing, got)
     swap = shuffle.core_copy(got.at[:, 1 - shuffle.core], from_mate)
@@ -563,27 +567,34 @@
     half = CHIPS * 8
     put_pair((h0, h1), pl.ds(0, half), got[:, shuffle.core].reshape(half, FEAT))
     w_out = split(w_out_ref[...])
+
+    def halo_step(at, carry):
+        rows = block_at(at, WIDE)
+        pre_ref[rows, :] += dot2(hot_rows(rep[rows, :], NEAR, half), pair_at((h0, h1), pl.ds(0, half)))
+        return carry
+
+    lax.fori_loop(0, EDGE // WIDE, halo_step, 0)
     swap.wait()
     put_pair((h0, h1), pl.ds(half, half), from_mate[...].reshape(half, FEAT))
 
     def edge_step(at, carry):
-        rows = block_at(at)
-        pre = pre_ref[rows, :] + dot2(hot_rows(rep[rows, :], NEAR, EDGE), (h0[...], h1[...]))
+        rows = block_at(at, WIDE)
+        pre = pre_ref[rows, :] + dot2(hot_rows(rep[rows, :], NEAR + half, half), pair_at((h0, h1), pl.ds(half, half)))
         pre_ref[rows, :] = pre
         normed, scale = norm(dot3(split(pre * sigmoid(pre)), w_out))
         normed_ref[rows, :] = normed
-        scale_ref[rows, :] = jnp.broadcast_to(scale, (BLOCK, 128))
+        scale_ref[rows, :] = jnp.broadcast_to(scale, (WIDE, 128))
         put_pair((n0, n1), rows, edge_ref[rows, :] + normed)
         return carry
 
-    lax.fori_loop(0, EDGE // BLOCK, edge_step, 0)
+    lax.fori_loop(0, EDGE // WIDE, edge_step, 0)
 
     def gather(at, carry):
-        rows = block_at(at)
-        agg_ref[rows, :] = dot2(hot_columns(recv_ref[...], at * BLOCK, BLOCK), (n0[...], n1[...]))
+        rows = block_at(at, WIDE)
+        agg_ref[rows, :] = dot2(hot_columns(recv_ref[...], at * WIDE, WIDE), (n0[...], n1[...]))
         return carry
 
-    lax.fori_loop(0, NEAR // BLOCK, gather, 0)
+    lax.fori_loop(0, NEAR // WIDE, gather, 0)
 
 
 def back_kernel(*refs):
@@ -599,7 +610,7 @@
     w_out = split(w_out_ref[...])
 
     def step(at, carry):
-        rows = block_at(at)
+        rows = block_at(at, WIDE)
         grad = cot_ref[rows, :] + dot2(hot_rows(recv_rep[rows, :], 0, NEAR), (a0[...], a1[...]))
         grad_edges_ref[rows, :] = grad
         tail = split(norm_back(grad, normed_ref[rows, :], scale_ref[rows, :1]))
@@ -609,27 +620,19 @@
         put_pair((d0, d1), rows, dot3(tail, w_out, NT) * (gate * (1.0 + pre * (1.0 - gate))))
         return carry
 
-    lax.fori_loop(0, EDGE // BLOCK, step, 0)
-
-    def halo_rows(first, at):
-        rows = dot2(hot_columns(send_ref[...], NEAR + first + at * BLOCK, BLOCK), (d0[...], d1[...]))
-        return rows.reshape(BLOCK // 8, 8, FEAT)
+    lax.fori_loop(0, EDGE // WIDE, step, 0)
 
     half = CHIPS * 8
 
-    def to_mate(at, carry):
-        for_mate[pl.ds(at * (BLOCK // 8), BLOCK // 8)] = halo_rows(half, at)
-        return carry
-
-    def to_pack(at, carry):
-        pack[pl.ds(at * (BLOCK // 8), BLOCK // 8), 0] = halo_rows(0, at)
-        return carry
-
-    lax.fori_loop(0, half // BLOCK, to_mate, 0)
+    def halo_rows(first):
+        rows = dot2(hot_columns(send_ref[...], NEAR + first, half), (d0[...], d1[...]))
+        return rows.reshape(CHIPS, 8, FEAT)
+
+    for_mate[...] = halo_rows(half)
     shuffle.wait_signals()
     swap = shuffle.core_copy(for_mate, pack.at[:, 1])
     swap.start()
-    lax.fori_loop(0, half // BLOCK, to_pack, 0)
+    pack[:, 0] = halo_rows(0)
     swap.wait()
     shuffle.send_chips(pack, back)
 
@@ -712,22 +715,50 @@
     ring.run(ring.SUM)
 
 
-def put_rows(ref, tiles, scale):
-    for at in range(FEAT // 128):
-        ref[:, at * 128 : (at + 1) * 128] = (tiles[:, at] * scale).reshape(-1, 128)
-
-
-def finish_kernel(edge_scale, node_scale, sum_ref, coarse_ref, in_ref, out_ref, node_in_ref, node_out_ref):
+def finish_kernel(pieces, sum_ref, coarse_ref, in_ref, out_ref, node_in_ref, node_out_ref, *rest):
+    rows, stores = rest[:-1], rest[-1]
+    outs = (coarse_ref, in_ref, out_ref, node_in_ref, node_out_ref)
     tiles = sum_ref.reshape(ROWS, 4, 8, 128)
-    for place, row in enumerate((EDGE_ROW, SEND_ROW, RECV_ROW)):
-        put_rows(in_ref.at[pl.ds(place * FEAT, FEAT)], tiles[row : row + 64], edge_scale)
-    put_rows(out_ref, tiles[OUT_ROW : OUT_ROW + 64], edge_scale)
-    whole = COARSE // 8
-    put_rows(coarse_ref.at[pl.ds(0, whole * 8)], tiles[COARSE_ROW : COARSE_ROW + whole], 1.0)
-    for at in range(FEAT // 128):
-        coarse_ref[whole * 8 :, at * 128 : (at + 1) * 128] = tiles[COARSE_ROW + whole, at][: COARSE - whole * 8]
-    put_rows(node_in_ref, tiles[0:128], node_scale)
-    put_rows(node_out_ref, tiles[128:192], node_scale)
+    puts = []
+    for at, (first, count, which, to, scale) in enumerate(pieces):
+        for column in range(FEAT // 128):
+            lanes = slice(column * 128, (column + 1) * 128)
+            whole = min(count, (outs[which].shape[0] - to) // 8)
+            value = tiles[first : first + whole, column] * scale
+            rows[which][to : to + whole * 8, lanes] = value.reshape(whole * 8, 128)
+            if whole < count:
+                rows[which][to + whole * 8 :, lanes] = tiles[first + whole, column][: COARSE - whole * 8] * scale
+        src, dst = rows[which], outs[which]
+        if count * 8 < src.shape[0]:
+            src, dst = src.at[pl.ds(to, count * 8)], dst.at[pl.ds(to, count * 8)]
+        puts.append(pltpu.make_async_copy(src, dst, stores.at[at]))
+        puts[-1].start()
+    for put in puts:
+        put.wait()
+
+
+def finish(summed, edge_scale, node_scale):
+    pieces = [
+        (0, 64, 3, 0, node_scale),
+        (64, 64, 3, FEAT, node_scale),
+        (128, 64, 4, 0, node_scale),
+        (OUT_ROW, 64, 2, 0, edge_scale),
+        (EDGE_ROW, 64, 1, 0, edge_scale),
+        (RECV_ROW, 64, 1, 2 * FEAT, edge_scale),
+        (COARSE_ROW, 81, 0, 0, 1.0),
+        (SEND_ROW, 64, 1, FEAT, edge_scale),
+    ]
+    any_spec = pl.BlockSpec(memory_space=pl.ANY)
+    sizes = (COARSE, 3 * FEAT, FEAT, 2 * FEAT, FEAT)
+    sem = pltpu.SemaphoreType.DMA((len(pieces),))
+    return pl.pallas_call(
+        functools.partial(finish_kernel, pieces),
+        out_shape=[f32_out(size, FEAT) for size in sizes],
+        in_specs=vmem_specs(1),
+        out_specs=[any_spec] * 5,
+        scratch_shapes=[pltpu.VMEM((size, FEAT), F32) for size in sizes] + [sem],
+        compiler_params=pltpu.CompilerParams(vmem_limit_bytes=24 << 20),
+    )(summed)
 
 
 def per_device(
@@ -809,15 +840,9 @@
     (summed,) = remote_call(
         sum_kernel, 4, [sum_out(3)], exchange_scratch(LINKS, 3), SUM_MIB, node, edge_out, in_edge, in_recv, coarse, in_send, few_direct
     )
-    grad_coarse, grad_in, grad_out, grad_node_in, grad_node_out = local_call(
-        functools.partial(
-            finish_kernel, 1.0 / math.sqrt(EDGE * peers), 1.0 / math.sqrt(FINE * peers + COARSE)
-        ),
-        [f32_out(COARSE, FEAT), f32_out(3 * FEAT, FEAT), f32_out(FEAT, FEAT), f32_out(2 * FEAT, FEAT), f32_out(FEAT, FEAT)],
-        [],
-        1e6,
-        summed,
-    )
+    edge_scale = 1.0 / math.sqrt(EDGE * peers)
+    node_scale = 1.0 / math.sqrt(FINE * peers + COARSE)
+    grad_coarse, grad_in, grad_out, grad_node_in, grad_node_out = finish(summed, edge_scale, node_scale)
     return grad_fine, grad_coarse, grad_edges, grad_in, grad_out, grad_node_in, grad_node_out
 
 

time: 231 us -> 225 us (0.974)
  Pallas kernels: 217 us -> 211 us
    pallas_call x4, Pallas kernels: 213 us -> 207 us  [remote_call(): pl.pallas_call(kernel, out_shape=outs, in_specs=vmem_specs(len(args)), ou...]
    unnamed x29 -> x31, local copies, waits for them, and re-layouts: 9.11 us -> 10.7 us
where the time goes in v1:
time: 225 us; the launch traced here: 224 us
  Pallas kernels  211 us (94%)
  local copies, waits for them, and re-layouts  11.9 us (5%)
    pallas_call x4, Pallas kernels, remote_call(): pl.pallas_call(kernel, out_shape=outs, in_specs=vmem_specs(len(args)), ou...  207 us
    unnamed x31, local copies, waits for them, and re-layouts  10.7 us

profile of v1, /device:TPU:1, one launch (start us, length us, event | category | flops | bytes accessed | tf_op | source)
XLA Modules:
  0.0 224.5 jit_solution(12620017415627198334)
XLA Ops:
  0.6 0.0 copy-start.1
  0.6 0.0 copy-start.12
  0.7 0.0 copy-start.13
  0.7 0.1 pad.4.clone
  0.8 0.8 compare_select_fusion
  1.6 0.8 pad_dynamic-slice_fusion
  2.3 0.0 copy-done.13
  2.3 0.1 copy.23
  2.4 0.1 reshape_reshape.3.refs_5_
  2.5 0.1 rev.3
  2.7 0.0 copy-start.8
  2.7 0.1 reshape.29.refs_11_
  2.9 0.0 copy-done.1
  2.9 0.0 copy-done.12
  2.9 0.0 copy-start.2
  2.9 0.2 maximum_maximum_fusion.refs_1_.refs_9_
  3.1 0.3 copy-done.8
  3.4 1.4 copy-done.2
  4.8 0.0 copy-start.4
  4.8 1.6 copy-done.4
  6.4 0.0 copy-start.6
  6.4 1.2 copy-done.6
  7.6 0.0 copy-start
  7.6 0.0 copy-start.3
  7.6 0.0 copy-start.5
  7.6 0.0 copy-start.7
  7.6 53.0 %shard_map.180 = (f32[1024,512]{1,0:T(8,128)S(1)}, f32[1024,512]{1,0:T(8,128)S(1)}, f32[1024,128]{1,0:T(8,128)S(1)}, f32[1024,512]{1,0:T(8,128)S(1)}) custom-call(f32[256,512]{1,0:T(8,128)S(1)} %copy-done.1, f32[1024,512]{1,0:T(8,128)S(1)} %maximum_maximum_fusion.refs_1_.refs_9_, f32[1024,512]{1,0:T(8,128)S(1)} %copy-done.4, f32[1536,512]{1,0:T(8,128)S(1)} %copy-done.2, ...), custom_call_target="tpu_custom_call" | custom-call | flops 30000001024 | bytes 30000000 | tf_op jit(solution)/shard_map/pallas_call | solution.py:334
  60.6 0.0 copy-done
  60.6 0.0 copy-start.9
  60.6 1.3 copy-done.9
  62.0 0.0 copy-start.10
  62.0 1.3 copy-done.10
  63.3 0.0 copy-done.3
  63.3 0.0 copy-done.5
  63.3 0.0 copy-done.7
  63.3 41.4 %shard_map.181 = (f32[1024,512]{1,0:T(8,128)S(1)}, f32[256,512]{1,0:T(8,128)S(1)}, f32[4,8,128]{2,1,0:T(8,128)S(1)}, f32[192,4,8,128]{3,2,1,0:T(8,128)S(1)}) custom-call(f32[1024,512]{1,0:T(8,128)S(1)} %get-tuple-element.27.refs_0_, f32[256,512]{1,0:T(8,128)S(1)} %copy-done.1, f32[256,512]{1,0:T(8,128)S(1)} %copy-done.7, ...), custom_call_target="tpu_custom_call" | custom-call | flops 30000001024 | bytes 30000000 | tf_op jit(solution)/shard_map/pallas_call | solution.py:334
  104.7 0.0 copy-start.11
  104.7 1.3 copy-done.11
  106.1 50.8 %shard_map.182 = (f32[1024,512]{1,0:T(8,128)S(1)}, f32[256,512]{1,0:T(8,128)S(1)}, f32[64,4,8,128]{3,2,1,0:T(8,128)S(1)}, f32[64,4,8,128]{3,2,1,0:T(8,128)S(1)},...) custom-call(f32[1024,512]{1,0:T(8,128)} %copy-done.11, ...), custom_call_target="tpu_custom_call" | custom-call | flops 30000001024 | bytes 30000000 | tf_op jit(solution)/shard_map/pallas_call | solution.py:334
  156.9 61.9 %shard_map.183.sum_ref = f32[6,128,3,8,128]{4,3,2,1,0:T(8,128)S(1)} custom-call(f32[192,4,8,128]{3,2,1,0:T(8,128)S(1)} %get-tuple-element.34.refs_0_, f32[64,4,8,128]{3,2,1,0:T(8,128)S(1)} %get-tuple-element.35.refs_1_, f32[64,4,8,128]{3,2,1,0:T(8,128)S(1)} %get-tuple-element.36.refs_2_, f32[64,4,8,128]{3,2,1,0:T(8,128)S(1)} %get-tuple-element.37.refs_3_, ...), custom_call_target="tpu_custom_call" | custom-call | flops 30000001024 | bytes 30000000 | tf_op jit(solution)/shard_map/pallas_call | solution.py:334
  218.8 3.6 %shard_map.184 = (f32[642,512]{1,0:T(8,128)}, f32[1536,512]{1,0:T(8,128)}, f32[512,512]{1,0:T(8,128)}, f32[1024,512]{1,0:T(8,128)}, f32[512,512]{1,0:T(8,128)}) custom-call(f32[6,128,3,8,128]{4,3,2,1,0:T(8,128)S(1)} %shard_map.183.sum_ref), custom_call_target="tpu_custom_call" | custom-call | tf_op jit(solution)/shard_map/pallas_call | solution.py:754
  222.3 0.8 copy.27
  223.1 1.3 copy.28
  (2 shorter events, 0.0 us)
Async XLA Ops:
  0.6 2.2 copy-start.1
  0.6 2.2 copy-start.12
  0.7 1.7 copy-start.13
  2.7 0.7 copy-start.8
  2.9 1.9 copy-start.2
  4.8 1.6 copy-start.4
  6.4 1.2 copy-start.6
  7.6 53.0 %copy-start = (f32[1024,512]{1,0:T(8,128)}, f32[1024,512]{1,0:T(8,128)S(1)}, u32[]{:S(2)}) copy-start(f32[1024,512]{1,0:T(8,128)S(1)} %maximum_maximum_fusion.refs_1_.refs_9_) | copy-start | bytes 6291460
  7.6 55.7 %copy-start.3 = (f32[1024,512]{1,0:T(8,128)S(1)}, f32[1024,512]{1,0:T(8,128)}, u32[]{:S(2)}) copy-start(f32[1024,512]{1,0:T(8,128)} %refs_5_.2) | copy-start | bytes 6291460
  7.6 55.7 %copy-start.5 = (f32[512,512]{1,0:T(8,128)S(1)}, f32[512,512]{1,0:T(8,128)}, u32[]{:S(2)}) copy-start(f32[512,512]{1,0:T(8,128)} %refs_6_.1) | copy-start | bytes 3145732
  7.6 55.7 %copy-start.7 = (f32[256,512]{1,0:T(8,128)S(1)}, f32[256,512]{1,0:T(8,128)}, u32[]{:S(2)}) copy-start(f32[256,512]{1,0:T(8,128)} %refs_2_.3) | copy-start | bytes 1572868
  60.6 1.3 copy-start.9
  62.0 1.3 copy-start.10
  104.7 1.3 copy-start.11

commit v2 on v1

--- a/solution.py
+++ b/solution.py
@@ -19,7 +19,7 @@
 BLOCK = 256
 LINKS = 6
 WIDE = 512
-FRONT_MIB, BACK_MIB, SUM_MIB = 38, 42, 30
+FRONT_MIB, BACK_MIB, SUM_MIB = 42, 42, 30
 
 NN = (((1,), (0,)), ((), ()))
 NT = (((1,), (1,)), ((), ()))
@@ -154,13 +154,15 @@
                 one=one, two=two, core=at_core, first=at_one, second=at_two, third=at_three, last=at_three + fourth
             )
 
-    def greet(self):
+    def signal(self):
         mates = [self.mate]
         mates += [self.peer(axis, shift) for axis in range(3) for shift in (1, 2, 3)]
         barrier = pltpu.get_barrier_semaphore()
         for mate in mates:
             pl.semaphore_signal(barrier, inc=1, device_id=(mate,), device_id_type=MESH)
-        pl.semaphore_wait(barrier, len(mates))
+
+    def wait_signals(self):
+        pl.semaphore_wait(pltpu.get_barrier_semaphore(), 10)
 
     def peer(self, axis, shift):
         return self.me + ((self.places[axis] + shift) % 4 - self.places[axis]) * STRIDES[axis]
@@ -297,13 +299,16 @@
     REDUCE = ("reduce_first", "reduce_kept", "reduce_second", "reduce_third", "reduce_fourth", "reduce_last")
     GATHER = ("gather_fourth", "gather_third", "gather_second", "gather_first", "gather_core", "gather_rest", "gather_last")
 
+    def stage(self, stage, *parts):
+        for part in parts:
+            getattr(self, stage)(part)
+
     def run(self, stages, beside=()):
         beside = list(beside)
         for stage in stages:
             if beside:
                 beside.pop(0)()
-            for part in range(len(self.specs)):
-                getattr(self, stage)(part)
+            self.stage(stage, *range(len(self.specs)))
         for work in beside:
             work()
 
@@ -371,12 +376,19 @@
         return self.product(self.grad, pair_at(self.w_in, pl.ds(first, FEAT)), NT)
 
 
+def few_rows(ref, me):
+    whole = COARSE // 8
+    rows = ref[pl.ds(pl.multiple_of(me % whole * 8, 8), 8), :]
+    rest = jnp.concatenate([ref[whole * 8 :, :], jnp.zeros((8 - COARSE % 8, FEAT), F32)], axis=0)
+    return jnp.where(me < whole, rows, jnp.where(me == whole, rest, 0.0))
+
+
 def node_kernel(*refs):
-    agg_ref, fine_ref, cot_ref, few_ref, few_cot_ref, w_in_ref, w_out_ref = refs[:7]
+    agg_ref, fine_ref, cot_ref, coarse_ref, coarse_cot_ref, w_in_ref, w_out_ref = refs[:7]
     grad_agg_ref, own_ref, direct_ref, node_ref = refs[7:11]
     buf, got, sends, recvs, full, wi0, wi1, wo0, wo1, total = refs[11:]
     ring = Exchange(FOUR_PARTS, buf, got, full, sends, recvs)
-    ring.greet()
+    ring.signal()
     for part, spec in enumerate(FOUR_PARTS):
         for device in range(128):
             first = FINE + 8 * device
@@ -384,13 +396,14 @@
                 buf[part, position(device, spec), 0] = agg_ref[first : first + 8, part * 128 : (part + 1) * 128]
             else:
                 buf[part, position(device, spec), 0] = jnp.zeros((8, 128), F32)
-        ring.start(part)
-    for part in range(4):
-        ring.start_kept(part)
+    ring.wait_signals()
+    ring.stage("start", *range(4))
+    ring.stage("start_kept", *range(4))
 
     wi, wo = (wi0, wi1), (wo0, wo1)
     fine = NodePass(dot3, wi, wo)
     few = NodePass(few_dot3, wi, wo)
+    few_feats, few_cot = few_rows(coarse_ref, ring.me), few_rows(coarse_cot_ref, ring.me)
 
     def cut_weights():
         wi0[...], wi1[...] = split(w_in_ref[...])
@@ -412,15 +425,15 @@
 
     few_agg = jnp.concatenate([buf[part, ring.spot[part]["last"], 0] for part in range(4)], axis=1)
     blank = jnp.zeros((8, FEAT), F32)
-    few.first(jnp.concatenate([few_ref[...], blank], axis=0), jnp.concatenate([few_agg, blank], axis=0))
+    few.first(jnp.concatenate([few_feats, blank], axis=0), jnp.concatenate([few_agg, blank], axis=0))
     few.second()
-    few.third(jnp.concatenate([few_cot_ref[...], blank], axis=0))
+    few.third(jnp.concatenate([few_cot, blank], axis=0))
     few_grad = few.back(FEAT)[:8]
     for part in range(4):
         full[part, ring.spot[part]["last"], 0] = few_grad[:, part * 128 : (part + 1) * 128]
 
     def few_back():
-        direct = few_cot_ref[...] + few.back(0)[:8]
+        direct = few_cot + few.back(0)[:8]
         for at in range(4):
             direct_ref[at] = direct[:, at * 128 : (at + 1) * 128]
 
@@ -443,7 +456,7 @@
             grad_agg_ref[first : first + 8, part * 128 : (part + 1) * 128] = full[part, position(device, spec), 0]
 
 
-def node_step(agg, fine, cot_fine, few, few_cot, w_in, w_out):
+def node_step(agg, fine, cot_fine, coarse, cot_coarse, w_in, w_out):
     half = pltpu.VMEM((2 * FEAT, FEAT), BF16)
     quarter = pltpu.VMEM((FEAT, FEAT), BF16)
     return remote_call(
@@ -456,8 +469,8 @@
         agg,
         fine,
         cot_fine,
-        few,
-        few_cot,
+        coarse,
+        cot_coarse,
         w_in,
         w_out,
     )
@@ -517,15 +530,33 @@
         return self.copy(src, dst, self.core_sends, self.core_recvs, self.mate)
 
 
+def halo_place(senders, core):
+    halo = senders - (FINE + COARSE)
+    source = jnp.right_shift(halo, 3)
+    kind = jnp.bitwise_and(source + core, 1)
+    place = NEAR + kind * (EDGE // 2) + jnp.right_shift(source, 1) * 8 + jnp.bitwise_and(halo, 7)
+    return jnp.where(halo < 0, senders, place)
+
+
 def front_kernel(*refs):
-    fine_ref, near_ref, edge_ref, w_ref, w_out_ref, list_ref, send_ref, recv_ref = refs[:8]
-    pre_ref, normed_ref, scale_ref, agg_ref = refs[8:12]
-    outgoing, got, from_mate, p0, p1, q0, q1, h0, h1, n0, n1, rep, recv_rep = refs[12:25]
-    shuffle = Shuffle(*refs[25:])
+    list_ref, sender_ref, recv_ref = refs[:3]
+    far_in, agg_ref, far_out = refs[3:8], refs[8], refs[9:13]
+    outgoing, got, from_mate, p0, p1, q0, q1, h0, h1, n0, n1, rep, recv_rep = refs[13:26]
+    near_ref, coarse_ref, w_ref, edge_ref, w_out_ref, pre_ref, normed_ref, scale_ref, send_ref, loads, stores = refs[26:37]
+    shuffle = Shuffle(*refs[37:])
+    places = (near_ref.at[pl.ds(0, FINE)], w_ref, coarse_ref, edge_ref, w_out_ref)
+    fetch = [pltpu.make_async_copy(src, dst, loads.at[at]) for at, (src, dst) in enumerate(zip(far_in, places))]
+    for copy in fetch:
+        copy.start()
+    results = (pre_ref, normed_ref, scale_ref, near_ref)
+    keep = [pltpu.make_async_copy(src, dst, stores.at[at]) for at, (src, dst) in enumerate(zip(results, far_out))]
     shuffle.signal()
+    rep[...] = spread(list_ref[...])
+    send_ref[...] = halo_place(sender_ref[...], shuffle.core)
+    for copy in fetch[:2]:
+        copy.wait()
     w_send = split(w_ref[FEAT : 2 * FEAT, :])
-    own = split(dot3(split(fine_ref[...]), w_send))
-    rep[...] = spread(list_ref[...])
+    own = split(dot3(split(near_ref[:FINE, :]), w_send))
 
     def request(at, carry):
         rows = block_at(at, WIDE)
@@ -540,6 +571,13 @@
     rep[...] = spread(send_ref[...])
     recv_rep[...] = spread(recv_ref[...])
     w_recv = split(w_ref[2 * FEAT :, :])
+    whole = COARSE // 8 * 8
+    for copy in fetch[2:]:
+        copy.wait()
+    near_ref[FINE : FINE + whole, :] = coarse_ref[:whole, :]
+    near_ref[FINE + whole :, :] = jnp.zeros((NEAR - FINE - whole, FEAT), F32)
+    near_ref[FINE + whole : FINE + COARSE, :] = coarse_ref[whole:, :]
+    keep[3].start()
 
     def project(at, carry):
         rows = block_at(at, WIDE)
@@ -588,6 +626,8 @@
         return carry
 
     lax.fori_loop(0, EDGE // WIDE, edge_step, 0)
+    for copy in keep[:3]:
+        copy.start()
 
     def gather(at, carry):
         rows = block_at(at, WIDE)
@@ -595,16 +635,19 @@
         return carry
 
     lax.fori_loop(0, NEAR // WIDE, gather, 0)
+    for copy in keep:
+        copy.wait()
 
 
 def back_kernel(*refs):
-    grad_agg_ref, cot_ref, pre_ref, normed_ref, scale_ref, w_out_ref, send_ref, recv_ref = refs[:8]
+    grad_agg_ref, cot_ref, pre_ref, normed_ref, scale_ref, w_out_ref, sender_ref, recv_ref = refs[:8]
     edge_ref, near_ref, w_ref, list_ref, direct_ref = refs[8:13]
     grad_edges_ref, grad_fine_ref, in_edge_ref, out_ref, in_recv_ref, coarse_ref, in_send_ref = refs[13:20]
     t0, t1, d0, d1, a0, a1, recv_rep, for_mate, pack, back = refs[20:30]
-    edge_total, tail_total, recv_total, send_total = refs[30:34]
-    shuffle = Shuffle(*refs[34:])
+    edge_total, tail_total, recv_total, send_total, send_ref = refs[30:35]
+    shuffle = Shuffle(*refs[35:])
     shuffle.signal()
+    send_ref[...] = halo_place(sender_ref[...], shuffle.core)
     recv_rep[...] = spread(recv_ref[...])
     a0[...], a1[...] = split(grad_agg_ref[...])
     w_out = split(w_out_ref[...])
@@ -680,7 +723,9 @@
     put_tiles(in_recv_ref, recv_total)
 
     shuffle.wait_chips(pack, back)
-    returned = split(back[...].reshape(EDGE, FEAT))
+    pack[:, 0] = back[:, shuffle.core]
+    pack[:, 1] = back[:, 1 - shuffle.core]
+    returned = split(pack[...].reshape(EDGE, FEAT))
     fine_sent = split(fine_sent + dot2(hot_columns(list_ref[...], 0, FINE), returned))
     grad_fine_ref[...] += dot3(fine_sent, w_send, NT)
     send_total[...] += dot3(split(near_ref[:FINE, :]), fine_sent, TN)
@@ -695,8 +740,7 @@
     sum_ref, buf, got, sends, recvs = refs[7:]
     flat = buf.reshape(ROWS * 4, 8, 128)
     ring = Exchange(ALL_PARTS, buf, got, sum_ref, sends, recvs)
-    ring.greet()
-    started = 0
+    ring.signal()
     row = 0
     for ref in (node_ref, out_ref, in_edge_ref, in_recv_ref, coarse_ref, in_send_ref):
         size = ref.shape[0]
@@ -707,11 +751,9 @@
         if row == SEND_ROW + 64:
             flat[row * 4 :] = jnp.zeros(((ROWS - row) * 4, 8, 128), F32)
             row = ROWS
-        while started < LINKS and (started + 1) * (ROWS // LINKS) <= row:
-            ring.start(started)
-            started += 1
-    for part in range(LINKS):
-        ring.start_kept(part)
+    ring.wait_signals()
+    ring.stage("start", *range(LINKS))
+    ring.stage("start_kept", *range(LINKS))
     ring.run(ring.SUM)
 
 
@@ -776,17 +818,9 @@
     cot_coarse,
     cot_edges,
 ):
-    me = lax.axis_index("patch")
     peers = lax.axis_size("patch")
-    core = me % 2
-    near_count = FINE + COARSE
-    send_list = send_rows.reshape(CHIPS, 2, 8)
-    back_list = jnp.where(core == 1, send_list[:, ::-1], send_list).reshape(1, EDGE)
-    send_list = send_list.reshape(1, EDGE)
-    halo = senders - near_count
-    source = halo // 8
-    halo_at = NEAR + (source % 2 != core) * (EDGE // 2) + source // 2 * 8 + halo % 8
-    send_at = jnp.where(senders < near_count, senders, halo_at).astype(jnp.int32).reshape(1, EDGE)
+    send_list = send_rows.reshape(1, EDGE)
+    send_at = senders.reshape(1, EDGE)
     recv_at = receivers.reshape(1, EDGE)
     half = pltpu.VMEM((EDGE, FEAT), BF16)
     index = pltpu.VMEM((EDGE, 128), jnp.int32)
@@ -797,31 +831,32 @@
     wide = f32_out(EDGE, FEAT)
     fine_out = f32_out(FINE, FEAT)
 
-    near = jnp.concatenate([fine_nodes, coarse_nodes, jnp.zeros((NEAR - near_count, FEAT), F32)], axis=0)
-    pre, normed, scale, agg = remote_call(
+    rows = pltpu.VMEM((EDGE, FEAT), F32)
+    rep_out = f32_out(EDGE, 128)
+    row_index = pltpu.VMEM((1, EDGE), jnp.int32)
+    hbm = pl.BlockSpec(memory_space=pltpu.HBM)
+    agg, pre, normed, scale, near = pl.pallas_call(
         front_kernel,
-        1,
-        [wide, wide, f32_out(EDGE, 128), wide],
-        [chip_rows, chip_rows, core_rows] + [half] * 8 + [index] * 2 + sems,
-        FRONT_MIB,
-        fine_nodes,
-        near,
-        edge_feats,
-        w_edge_in,
-        w_edge_out,
-        send_list,
-        send_at,
-        recv_at,
+        out_shape=[wide, wide, wide, rep_out, wide],
+        in_specs=vmem_specs(3) + [hbm] * 5,
+        out_specs=vmem_specs(1) + [hbm] * 4,
+        scratch_shapes=[chip_rows, chip_rows, core_rows]
+        + [half] * 8
+        + [index] * 2
+        + [rows, pltpu.VMEM((COARSE, FEAT), F32), pltpu.VMEM((3 * FEAT, FEAT), F32), rows, square]
+        + [rows, rows, pltpu.VMEM((EDGE, 128), F32), row_index]
+        + [pltpu.SemaphoreType.DMA((5,)), pltpu.SemaphoreType.DMA((4,))]
+        + sems,
+        compiler_params=pltpu.CompilerParams(collective_id=1, has_side_effects=True, vmem_limit_bytes=FRONT_MIB << 20),
+    )(send_list, send_at, recv_at, fine_nodes, w_edge_in, coarse_nodes, edge_feats, w_edge_out)
+    grad_agg, direct, few_direct, node = node_step(
+        agg, fine_nodes, cot_fine, coarse_nodes, cot_coarse, w_node_in, w_node_out
     )
-    blank = jnp.zeros((8 * peers - COARSE, FEAT), F32)
-    few = lax.dynamic_slice(jnp.concatenate([coarse_nodes, blank], axis=0), (me * 8, 0), (8, FEAT))
-    few_cot = lax.dynamic_slice(jnp.concatenate([cot_coarse, blank], axis=0), (me * 8, 0), (8, FEAT))
-    grad_agg, direct, few_direct, node = node_step(agg, fine_nodes, cot_fine, few, few_cot, w_node_in, w_node_out)
     grad_edges, grad_fine, in_edge, edge_out, in_recv, coarse, in_send = remote_call(
         back_kernel,
         3,
         [wide, fine_out, TILES, TILES, TILES, f32_out(96, 4, 8, 128), TILES],
-        [half] * 6 + [index, core_rows, chip_rows, chip_rows] + [square] * 4 + sems,
+        [half] * 6 + [index, core_rows, chip_rows, chip_rows] + [square] * 4 + [row_index] + sems,
         BACK_MIB,
         grad_agg,
         cot_edges,
@@ -834,7 +869,7 @@
         edge_feats,
         near,
         w_edge_in,
-        back_list,
+        send_list,
         direct,
     )
     (summed,) = remote_call(

time: 225 us -> 225 us (level)
    pallas_call x0 -> x1, Pallas kernels: none -> 54.1 us  [per_device(): pl.pallas_call(front_kernel, out_shape=[wide, wide, wide, rep_out, wide],...]
    pallas_call x4 -> x3, Pallas kernels: 207 us -> 154 us  [remote_call(): pl.pallas_call(kernel, out_shape=outs, in_specs=vmem_specs(len(args)), ou...]
    unnamed x31 -> x43, local copies, waits for them, and re-layouts: 10.7 us -> 12.2 us
where the time goes in v2:
time: 225 us; the launch traced here: 224 us
  Pallas kernels  211 us (94%)
  local copies, waits for them, and re-layouts  12.3 us (5%)
    pallas_call x3, Pallas kernels, remote_call(): pl.pallas_call(kernel, out_shape=outs, in_specs=vmem_specs(len(args)), ou...  154 us
    pallas_call x1, Pallas kernels, per_device(): pl.pallas_call(front_kernel, out_shape=[wide, wide, wide, rep_out, wide],...  54.1 us
    unnamed x43, local copies, waits for them, and re-layouts  12.2 us

profile of v2, /device:TPU:1, one launch (start us, length us, event | category | flops | bytes accessed | tf_op | source)
XLA Modules:
  0.0 224.3 jit_solution(7389698894245021563)
XLA Ops:
  0.6 0.8 copy.21
  1.4 0.1 reshape.23.refs_0_.refs_11_
  1.5 0.0 copy-start
  1.5 1.3 copy-done
  2.8 0.0 copy-start.2
  2.8 1.2 copy-done.2
  4.1 0.0 copy-start.4
  4.1 1.0 copy-done.4
  5.1 0.0 copy-start.6
  5.1 0.7 copy-done.6
  5.8 0.0 copy-start.8
  5.8 0.7 copy-done.8
  6.5 0.0 copy-start.1
  6.5 0.0 copy-start.5
  6.5 0.0 copy-start.10
  6.5 0.0 copy-start.14
  6.5 0.0 copy-start.15
  6.5 0.0 copy-start.16
  6.5 54.1 %shard_map.180 = (f32[1024,512]{1,0:T(8,128)S(1)}, f32[1024,512]{1,0:T(8,128)S(1)}, f32[1024,512]{1,0:T(8,128)S(1)}, f32[1024,128]{1,0:T(8,128)S(1)}, f32[1024,512]{1,0:T(8,128)S(1)}) custom-call(s32[1,1024]{1,0:T(1,128)S(1)} %reshape.23.refs_0_.refs_11_, s32[1,1024]{1,0:T(1,128)S(1)} %bitcast.2, s32[1,1024]{1,0:T(1,128)S(1)} %bitcast.4, ...), custom_call_target="tpu_custom_call" | custom-call | tf_op jit(solution)/shard_map/pallas_call | solution.py:838
  60.6 0.0 copy-start.11
  60.6 1.3 copy-done.11
  61.9 0.0 copy-start.12
  61.9 0.0 copy-start.13
  61.9 0.0 copy-done.1
  61.9 0.0 copy-done.5
  61.9 0.0 copy-done.10
  62.0 0.0 copy-done.14
  62.0 0.0 copy-done.15
  62.0 0.0 copy-done.16
  62.0 0.0 copy-start.3
  62.0 0.0 copy-start.7
  62.0 0.0 copy-start.9
  62.0 41.4 %shard_map.181 = (f32[1024,512]{1,0:T(8,128)S(1)}, f32[256,512]{1,0:T(8,128)S(1)}, f32[4,8,128]{2,1,0:T(8,128)S(1)}, f32[192,4,8,128]{3,2,1,0:T(8,128)S(1)}) custom-call(f32[1024,512]{1,0:T(8,128)S(1)} %get-tuple-element.28.refs_0_, f32[256,512]{1,0:T(8,128)S(1)} %copy-done.5, f32[256,512]{1,0:T(8,128)S(1)} %copy-done.16, f32[642,512]{1,0:T(8,128)S(1)} %copy-done.1, ...), custom_call_target="tpu_custom_call" | custom-call | flops 30000001024 | bytes 30000000 | tf_op jit(solution)/shard_map/pallas_call | solution.py:339
  103.4 0.0 copy-done.12
  103.5 0.0 copy-done.13
  103.5 0.0 copy-start.17
  103.5 1.7 copy-done.17
  105.1 0.0 copy-start.19
  105.1 1.3 copy-done.19
  106.5 0.0 copy-done.3
  106.5 0.0 copy-done.7
  106.5 0.0 copy-done.9
  106.5 50.9 %shard_map.182 = (f32[1024,512]{1,0:T(8,128)S(1)}, f32[256,512]{1,0:T(8,128)S(1)}, f32[64,4,8,128]{3,2,1,0:T(8,128)S(1)}, f32[64,4,8,128]{3,2,1,0:T(8,128)S(1)},...) custom-call(f32[1024,512]{1,0:T(8,128)} %copy-done.19, ...), custom_call_target="tpu_custom_call" | custom-call | flops 30000001024 | bytes 30000000 | tf_op jit(solution)/shard_map/pallas_call | solution.py:339
  157.4 0.0 copy-done.18
  157.4 61.3 %shard_map.183.sum_ref = f32[6,128,3,8,128]{4,3,2,1,0:T(8,128)S(1)} custom-call(f32[192,4,8,128]{3,2,1,0:T(8,128)S(1)} %copy-done.18, f32[64,4,8,128]{3,2,1,0:T(8,128)S(1)} %get-tuple-element.37.refs_1_, f32[64,4,8,128]{3,2,1,0:T(8,128)S(1)} %get-tuple-element.38.refs_2_, f32[64,4,8,128]{3,2,1,0:T(8,128)S(1)} %get-tuple-element.39.refs_3_, ...), custom_call_target="tpu_custom_call" | custom-call | flops 30000001024 | bytes 30000000 | tf_op jit(solution)/shard_map/pallas_call | solution.py:339
  218.6 3.6 %shard_map.184 = (f32[642,512]{1,0:T(8,128)}, f32[1536,512]{1,0:T(8,128)}, f32[512,512]{1,0:T(8,128)}, f32[1024,512]{1,0:T(8,128)}, f32[512,512]{1,0:T(8,128)}) custom-call(f32[6,128,3,8,128]{4,3,2,1,0:T(8,128)S(1)} %shard_map.183.sum_ref), custom_call_target="tpu_custom_call" | custom-call | tf_op jit(solution)/shard_map/pallas_call | solution.py:796
  222.2 0.8 copy.24
  223.0 1.3 copy.25
  (1 shorter events, 0.0 us)
Async XLA Ops:
  1.5 1.3 copy-start
  2.8 1.2 copy-start.2
  4.1 1.0 copy-start.4
  5.1 0.7 copy-start.6
  5.8 0.7 copy-start.8
  6.5 55.5 %copy-start.1 = (f32[642,512]{1,0:T(8,128)S(1)}, f32[642,512]{1,0:T(8,128)}, u32[]{:S(2)}) copy-start(f32[642,512]{1,0:T(8,128)} %refs_3_.3) | copy-start | bytes 3944452
  6.5 55.5 %copy-start.5 = (f32[256,512]{1,0:T(8,128)S(1)}, f32[256,512]{1,0:T(8,128)}, u32[]{:S(2)}) copy-start(f32[256,512]{1,0:T(8,128)} %refs_1_.2) | copy-start | bytes 1572868
  6.5 55.5 %copy-start.10 = (f32[1024,512]{1,0:T(8,128)S(1)}, f32[1024,512]{1,0:T(8,128)}, u32[]{:S(2)}) copy-start(f32[1024,512]{1,0:T(8,128)} %refs_5_.4) | copy-start | bytes 6291460
  6.5 55.5 %copy-start.14 = (f32[642,512]{1,0:T(8,128)S(1)}, f32[642,512]{1,0:T(8,128)}, u32[]{:S(2)}) copy-start(f32[642,512]{1,0:T(8,128)} %refs_4_.3) | copy-start | bytes 3944452
  6.5 55.5 %copy-start.15 = (f32[512,512]{1,0:T(8,128)S(1)}, f32[512,512]{1,0:T(8,128)}, u32[]{:S(2)}) copy-start(f32[512,512]{1,0:T(8,128)} %refs_6_.3) | copy-start | bytes 3145732
  6.5 55.5 %copy-start.16 = (f32[256,512]{1,0:T(8,128)S(1)}, f32[256,512]{1,0:T(8,128)}, u32[]{:S(2)}) copy-start(f32[256,512]{1,0:T(8,128)} %refs_2_.1) | copy-start | bytes 1572868
  60.6 1.3 copy-start.11
  61.9 41.5 %copy-start.12 = (f32[1024,512]{1,0:T(8,128)}, f32[1024,512]{1,0:T(8,128)S(1)}, u32[]{:S(2)}) copy-start(f32[1024,512]{1,0:T(8,128)S(1)} %get-tuple-element.31.refs_3_) | copy-start | bytes 6291460
  61.9 41.5 %copy-start.13 = (f32[1024,512]{1,0:T(8,128)}, f32[1024,512]{1,0:T(8,128)S(1)}, u32[]{:S(2)}) copy-start(f32[1024,512]{1,0:T(8,128)S(1)} %get-tuple-element.33.refs_9_) | copy-start | bytes 6291460
  62.0 44.5 %copy-start.3 = (f32[512,512]{1,0:T(8,128)S(1)}, f32[512,512]{1,0:T(8,128)}, u32[]{:S(2)}) copy-start(f32[512,512]{1,0:T(8,128)} %refs_5_.5) | copy-start | bytes 3145732
  62.0 44.5 %copy-start.7 = (s32[1024]{0:T(1024)S(1)}, s32[1024]{0:T(1024)}, u32[]{:S(2)}) copy-start(s32[1024]{0:T(1024)} %param.16) | copy-start | bytes 12292
  62.0 44.5 %copy-start.9 = (s32[1024]{0:T(1024)S(1)}, s32[1024]{0:T(1024)}, u32[]{:S(2)}) copy-start(s32[1024]{0:T(1024)} %param.17) | copy-start | bytes 12292
  103.5 1.7 copy-start.17
  105.1 1.3 copy-start.19
  106.5 50.9 %copy-start.18 = (f32[192,4,8,128]{3,2,1,0:T(8,128)S(1)}, f32[192,4,8,128]{3,2,1,0:T(8,128)}, u32[]{:S(2)}) copy-start(f32[192,4,8,128]{3,2,1,0:T(8,128)} %copy-done.17) | copy-start | bytes 9437188

commit v3 on v2

--- a/solution.py
+++ b/solution.py
@@ -19,7 +19,7 @@
 BLOCK = 256
 LINKS = 6
 WIDE = 512
-FRONT_MIB, BACK_MIB, SUM_MIB = 42, 42, 30
+FRONT_MIB, BACK_MIB, SUM_MIB = 60, 42, 30
 
 NN = (((1,), (0,)), ((), ()))
 NT = (((1,), (1,)), ((), ()))
@@ -757,11 +757,16 @@
     ring.run(ring.SUM)
 
 
-def finish_kernel(pieces, sum_ref, coarse_ref, in_ref, out_ref, node_in_ref, node_out_ref, *rest):
-    rows, stores = rest[:-1], rest[-1]
+def finish_kernel(pieces, sum_ref, edges_ref, fine_ref, coarse_ref, in_ref, out_ref, node_in_ref, node_out_ref, edges_out, fine_out, *rest):
+    rows, stores, passes = rest[:-2], rest[-2], rest[-1]
     outs = (coarse_ref, in_ref, out_ref, node_in_ref, node_out_ref)
     tiles = sum_ref.reshape(ROWS, 4, 8, 128)
-    puts = []
+    puts = [
+        pltpu.make_async_copy(edges_ref, edges_out, passes.at[0]),
+        pltpu.make_async_copy(fine_ref, fine_out, passes.at[1]),
+    ]
+    for put in puts:
+        put.start()
     for at, (first, count, which, to, scale) in enumerate(pieces):
         for column in range(FEAT // 128):
             lanes = slice(column * 128, (column + 1) * 128)
@@ -779,7 +784,7 @@
         put.wait()
 
 
-def finish(summed, edge_scale, node_scale):
+def finish(summed, grad_edges, grad_fine, edge_scale, node_scale):
     pieces = [
         (0, 64, 3, 0, node_scale),
         (64, 64, 3, FEAT, node_scale),
@@ -795,12 +800,12 @@
     sem = pltpu.SemaphoreType.DMA((len(pieces),))
     return pl.pallas_call(
         functools.partial(finish_kernel, pieces),
-        out_shape=[f32_out(size, FEAT) for size in sizes],
-        in_specs=vmem_specs(1),
-        out_specs=[any_spec] * 5,
-        scratch_shapes=[pltpu.VMEM((size, FEAT), F32) for size in sizes] + [sem],
+        out_shape=[f32_out(size, FEAT) for size in sizes + (EDGE, FINE)],
+        in_specs=vmem_specs(1) + [any_spec] * 2,
+        out_specs=[any_spec] * 7,
+        scratch_shapes=[pltpu.VMEM((size, FEAT), F32) for size in sizes] + [sem, pltpu.SemaphoreType.DMA((2,))],
         compiler_params=pltpu.CompilerParams(vmem_limit_bytes=24 << 20),
-    )(summed)
+    )(summed, grad_edges, grad_fine)
 
 
 def per_device(
@@ -877,7 +882,9 @@
     )
     edge_scale = 1.0 / math.sqrt(EDGE * peers)
     node_scale = 1.0 / math.sqrt(FINE * peers + COARSE)
-    grad_coarse, grad_in, grad_out, grad_node_in, grad_node_out = finish(summed, edge_scale, node_scale)
+    grad_coarse, grad_in, grad_out, grad_node_in, grad_node_out, grad_edges, grad_fine = finish(
+        summed, grad_edges, grad_fine, edge_scale, node_scale
+    )
     return grad_fine, grad_coarse, grad_edges, grad_in, grad_out, grad_node_in, grad_node_out
 
 

time: 225 us -> 222 us (0.987)
  local copies, waits for them, and re-layouts: 12.3 us -> 7.99 us
    unnamed x43 -> x27, local copies, waits for them, and re-layouts: 12.2 us -> 7.3 us
where the time goes in v3:
time: 222 us
  Pallas kernels  213 us (96%)
  local copies, waits for them, and re-layouts  7.99 us (4%)
    pallas_call x3, Pallas kernels, remote_call(): pl.pallas_call(kernel, out_shape=outs, in_specs=vmem_specs(len(args)), ou...  153 us
    pallas_call x1, Pallas kernels, per_device(): pl.pallas_call(front_kernel, out_shape=[wide, wide, wide, rep_out, wide],...  55.3 us
    unnamed x27, local copies, waits for them, and re-layouts  7.3 us

profile of v3, /device:TPU:1, one launch (start us, length us, event | category | flops | bytes accessed | tf_op | source)
XLA Modules:
  0.0 222.0 jit_solution(17961624317788767118)
XLA Ops:
  0.6 0.8 copy.21
  1.4 0.7 reshape.23.refs_0_.refs_11_
  2.1 0.0 copy-start
  2.1 0.0 copy-start.2
  2.1 0.0 copy-start.6
  2.1 55.3 %shard_map.180 = (f32[1024,512]{1,0:T(8,128)}, f32[1024,512]{1,0:T(8,128)}, f32[1024,512]{1,0:T(8,128)}, f32[1024,128]{1,0:T(8,128)}, f32[1024,512]{1,0:T(8,128)}) custom-call(s32[1,1024]{1,0:T(1,128)} %reshape.23.refs_0_.refs_11_, s32[1,1024]{1,0:T(1,128)} %bitcast.2, s32[1,1024]{1,0:T(1,128)} %bitcast.4, f32[256,512]{1,0:T(8,128)} %refs_1_.2, ...), custom_call_target="tpu_custom_call" | custom-call | tf_op jit(solution)/shard_map/pallas_call | solution.py:843
  57.5 0.0 copy-done
  57.5 0.0 copy-done.2
  57.5 0.0 copy-done.6
  57.5 0.0 copy-start.7
  57.5 1.6 copy-done.7
  59.1 0.0 copy-start.8
  59.1 1.3 copy-done.8
  60.4 0.0 copy-start.9
  60.4 1.2 copy-done.9
  61.6 0.0 copy-start.10
  61.6 1.0 copy-done.10
  62.7 0.0 copy-start.1
  62.7 0.0 copy-start.3
  62.7 0.0 copy-start.4
  62.7 0.0 copy-start.5
  62.7 0.0 copy-start.11
  62.7 41.4 %shard_map.181 = (f32[1024,512]{1,0:T(8,128)S(1)}, f32[256,512]{1,0:T(8,128)S(1)}, f32[4,8,128]{2,1,0:T(8,128)S(1)}, f32[192,4,8,128]{3,2,1,0:T(8,128)S(1)}) custom-call(f32[1024,512]{1,0:T(8,128)S(1)} %copy-done.7, f32[256,512]{1,0:T(8,128)S(1)} %copy-done.2, f32[256,512]{1,0:T(8,128)S(1)} %copy-done.10, f32[642,512]{1,0:T(8,128)S(1)} %copy-done, ...), custom_call_target="tpu_custom_call" | custom-call | flops 30000001024 | bytes 30000000 | tf_op jit(solution)/shard_map/pallas_call | solution.py:339
  104.1 0.0 copy-start.12
  104.1 1.3 copy-done.12
  105.5 0.0 copy-done.1
  105.5 0.0 copy-done.3
  105.5 0.0 copy-done.4
  105.5 0.0 copy-done.5
  105.5 0.0 copy-done.11
  105.5 50.8 %shard_map.182 = (f32[1024,512]{1,0:T(8,128)S(1)}, f32[256,512]{1,0:T(8,128)S(1)}, f32[64,4,8,128]{3,2,1,0:T(8,128)S(1)}, f32[64,4,8,128]{3,2,1,0:T(8,128)S(1)},...) custom-call(f32[1024,512]{1,0:T(8,128)} %copy-done.12, ...), custom_call_target="tpu_custom_call" | custom-call | flops 30000001024 | bytes 30000000 | tf_op jit(solution)/shard_map/pallas_call | solution.py:339
  156.3 61.2 %shard_map.183.sum_ref = f32[6,128,3,8,128]{4,3,2,1,0:T(8,128)S(1)} custom-call(f32[192,4,8,128]{3,2,1,0:T(8,128)S(1)} %get-tuple-element.31.refs_0_, f32[64,4,8,128]{3,2,1,0:T(8,128)S(1)} %get-tuple-element.38.refs_1_, f32[64,4,8,128]{3,2,1,0:T(8,128)S(1)} %get-tuple-element.39.refs_2_, f32[64,4,8,128]{3,2,1,0:T(8,128)S(1)} %get-tuple-element.40.refs_3_, ...), custom_call_target="tpu_custom_call" | custom-call | flops 30000001024 | bytes 30000000 | tf_op jit(solution)/shard_map/pallas_call | solution.py:339
  217.5 4.3 %shard_map.184 = (f32[642,512]{1,0:T(8,128)}, f32[1536,512]{1,0:T(8,128)}, f32[512,512]{1,0:T(8,128)}, f32[1024,512]{1,0:T(8,128)}, f32[512,512]{1,0:T(8,128)}, /*index=5*/f32[1024,512]{1,0:T(8,128)}, f32[256,512]{1,0:T(8,128)}) custom-call(f32[6,128,3,8,128]{4,3,2,1,0:T(8,128)S(1)} %shard_map.183.sum_ref, f32[1024,512]{1,0:T(8,128)S(1)} %get-tuple-element.44.edges_ref, ...), custom_call_target="tpu_custom_call" | custom-call | tf_op jit(solution)/shard_map/pallas_call | solution.py:801
Async XLA Ops:
  2.1 55.3 %copy-start = (f32[642,512]{1,0:T(8,128)S(1)}, f32[642,512]{1,0:T(8,128)}, u32[]{:S(2)}) copy-start(f32[642,512]{1,0:T(8,128)} %refs_3_.3) | copy-start | bytes 3944452
  2.1 55.3 %copy-start.2 = (f32[256,512]{1,0:T(8,128)S(1)}, f32[256,512]{1,0:T(8,128)}, u32[]{:S(2)}) copy-start(f32[256,512]{1,0:T(8,128)} %refs_1_.2) | copy-start | bytes 1572868
  2.1 55.4 %copy-start.6 = (f32[1024,512]{1,0:T(8,128)S(1)}, f32[1024,512]{1,0:T(8,128)}, u32[]{:S(2)}) copy-start(f32[1024,512]{1,0:T(8,128)} %refs_5_.4) | copy-start | bytes 6291460
  57.5 1.6 copy-start.7
  59.1 1.3 copy-start.8
  60.4 1.2 copy-start.9
  61.6 1.0 copy-start.10
  62.7 42.8 %copy-start.1 = (f32[512,512]{1,0:T(8,128)S(1)}, f32[512,512]{1,0:T(8,128)}, u32[]{:S(2)}) copy-start(f32[512,512]{1,0:T(8,128)} %refs_5_.5) | copy-start | bytes 3145732
  62.7 42.8 %copy-start.3 = (s32[1,1024]{1,0:T(1,128)S(1)}, s32[1,1024]{1,0:T(1,128)}, u32[]{:S(2)}) copy-start(s32[1,1024]{1,0:T(1,128)} %reshape.23.refs_0_.refs_11_) | copy-start | bytes 12292
  62.7 42.8 %copy-start.4 = (s32[1024]{0:T(1024)S(1)}, s32[1024]{0:T(1024)}, u32[]{:S(2)}) copy-start(s32[1024]{0:T(1024)} %param.16) | copy-start | bytes 12292
  62.7 42.8 %copy-start.5 = (s32[1024]{0:T(1024)S(1)}, s32[1024]{0:T(1024)}, u32[]{:S(2)}) copy-start(s32[1024]{0:T(1024)} %param.17) | copy-start | bytes 12292
  62.7 42.8 %copy-start.11 = (f32[1024,128]{1,0:T(8,128)S(1)}, f32[1024,128]{1,0:T(8,128)}, u32[]{:S(2)}) copy-start(f32[1024,128]{1,0:T(8,128)} %get-tuple-element.35.refs_4_) | copy-start | bytes 1572868
  104.1 1.3 copy-start.12

commit v4 on v3

--- a/solution.py
+++ b/solution.py
@@ -19,7 +19,7 @@
 BLOCK = 256
 LINKS = 6
 WIDE = 512
-FRONT_MIB, BACK_MIB, SUM_MIB = 60, 42, 30
+FRONT_MIB, BACK_MIB, SUM_MIB = 57, 41, 30
 
 NN = (((1,), (0,)), ((), ()))
 NT = (((1,), (1,)), ((), ()))
@@ -488,6 +488,7 @@
         self.mate = self.me + 1 - 2 * self.core
 
     def other(self, step):
+        step = step * 27 % CHIPS
         z, x, y = ((place + step // span) % 4 for place, span in zip(self.places, (16, 4, 1)))
         return z * 16 + x * 4 + y
 

time: 222 us -> 204 us (0.919)
  Pallas kernels: 213 us -> 198 us
  local copies, waits for them, and re-layouts: 7.99 us -> 4.77 us
    pallas_call x3, Pallas kernels: 153 us -> 145 us  [remote_call(): pl.pallas_call(kernel, out_shape=outs, in_specs=vmem_specs(len(args)), ou...]
    pallas_call x1, Pallas kernels: 55.3 us -> 48.7 us  [per_device(): pl.pallas_call(front_kernel, out_shape=[wide, wide, wide, rep_out, wide],...]
    unnamed x27 -> x29, local copies, waits for them, and re-layouts: 7.3 us -> 4.08 us
where the time goes in v4:
time: 204 us
  Pallas kernels  198 us (97%)
  local copies, waits for them, and re-layouts  4.77 us (2%)
    pallas_call x3, Pallas kernels, remote_call(): pl.pallas_call(kernel, out_shape=outs, in_specs=vmem_specs(len(args)), ou...  145 us
    pallas_call x1, Pallas kernels, per_device(): pl.pallas_call(front_kernel, out_shape=[wide, wide, wide, rep_out, wide],...  48.7 us
    pallas_call x1, Pallas kernels, finish(): pl.pallas_call(functools.partial(finish_kernel, pieces), out_shape=[f32_o...  4.28 us
    unnamed x29, local copies, waits for them, and re-layouts  4.08 us

profile of v4, /device:TPU:1, one launch (start us, length us, event | category | flops | bytes accessed | tf_op | source)
XLA Modules:
  0.0 203.6 jit_solution(10948830242480886280)
XLA Ops:
  0.6 0.8 copy.21
  1.4 0.7 reshape.23.refs_0_.refs_11_
  2.1 0.0 copy-start
  2.1 0.0 copy-start.2
  2.1 0.0 copy-start.6
  2.1 0.0 copy-start.8
  2.1 0.0 copy-start.9
  2.1 0.0 copy-start.10
  2.1 48.7 %shard_map.180 = (f32[1024,512]{1,0:T(8,128)}, f32[1024,512]{1,0:T(8,128)}, f32[1024,512]{1,0:T(8,128)}, f32[1024,128]{1,0:T(8,128)}, f32[1024,512]{1,0:T(8,128)}) custom-call(s32[1,1024]{1,0:T(1,128)} %reshape.23.refs_0_.refs_11_, s32[1,1024]{1,0:T(1,128)} %bitcast.2, s32[1,1024]{1,0:T(1,128)} %bitcast.4, f32[256,512]{1,0:T(8,128)} %refs_1_.2, ...), custom_call_target="tpu_custom_call" | custom-call | tf_op jit(solution)/shard_map/pallas_call | solution.py:844
  50.8 0.0 copy-done
  50.8 0.0 copy-done.2
  50.8 0.0 copy-done.6
  50.9 0.0 copy-done.8
  50.9 0.0 copy-done.9
  50.9 0.0 copy-done.10
  50.9 0.0 copy-start.7
  50.9 1.6 copy-done.7
  52.5 0.0 copy-start.1
  52.5 0.0 copy-start.3
  52.5 0.0 copy-start.4
  52.5 0.0 copy-start.5
  52.5 0.0 copy-start.11
  52.5 40.9 %shard_map.181 = (f32[1024,512]{1,0:T(8,128)S(1)}, f32[256,512]{1,0:T(8,128)S(1)}, f32[4,8,128]{2,1,0:T(8,128)S(1)}, f32[192,4,8,128]{3,2,1,0:T(8,128)S(1)}) custom-call(f32[1024,512]{1,0:T(8,128)S(1)} %copy-done.7, f32[256,512]{1,0:T(8,128)S(1)} %copy-done.2, f32[256,512]{1,0:T(8,128)S(1)} %copy-done.10, f32[642,512]{1,0:T(8,128)S(1)} %copy-done, ...), custom_call_target="tpu_custom_call" | custom-call | flops 30000001024 | bytes 30000000 | tf_op jit(solution)/shard_map/pallas_call | solution.py:339
  93.4 0.0 copy-start.12
  93.4 1.7 copy-done.12
  95.1 0.0 copy-done.1
  95.1 0.0 copy-done.3
  95.1 0.0 copy-done.4
  95.1 0.0 copy-done.5
  95.1 0.0 copy-done.11
  95.1 0.0 copy-start.13
  95.1 44.7 %shard_map.182 = (f32[1024,512]{1,0:T(8,128)S(1)}, f32[256,512]{1,0:T(8,128)S(1)}, f32[64,4,8,128]{3,2,1,0:T(8,128)S(1)}, f32[64,4,8,128]{3,2,1,0:T(8,128)S(1)},...) custom-call(f32[1024,512]{1,0:T(8,128)S(1)} %get-tuple-element.32.refs_0_, ...), custom_call_target="tpu_custom_call" | custom-call | flops 30000001024 | bytes 30000000 | tf_op jit(solution)/shard_map/pallas_call | solution.py:339
  139.8 0.0 copy-done.13
  139.8 59.4 %shard_map.183.sum_ref = f32[6,128,3,8,128]{4,3,2,1,0:T(8,128)S(1)} custom-call(f32[192,4,8,128]{3,2,1,0:T(8,128)S(1)} %copy-done.13, f32[64,4,8,128]{3,2,1,0:T(8,128)S(1)} %get-tuple-element.38.refs_1_, f32[64,4,8,128]{3,2,1,0:T(8,128)S(1)} %get-tuple-element.39.refs_2_, f32[64,4,8,128]{3,2,1,0:T(8,128)S(1)} %get-tuple-element.40.refs_3_, ...), custom_call_target="tpu_custom_call" | custom-call | flops 30000001024 | bytes 30000000 | tf_op jit(solution)/shard_map/pallas_call | solution.py:339
  199.1 4.3 %shard_map.184 = (f32[642,512]{1,0:T(8,128)}, f32[1536,512]{1,0:T(8,128)}, f32[512,512]{1,0:T(8,128)}, f32[1024,512]{1,0:T(8,128)}, f32[512,512]{1,0:T(8,128)}, /*index=5*/f32[1024,512]{1,0:T(8,128)}, f32[256,512]{1,0:T(8,128)}) custom-call(f32[6,128,3,8,128]{4,3,2,1,0:T(8,128)S(1)} %shard_map.183.sum_ref, f32[1024,512]{1,0:T(8,128)S(1)} %get-tuple-element.44.edges_ref, ...), custom_call_target="tpu_custom_call" | custom-call | tf_op jit(solution)/shard_map/pallas_call | solution.py:802
Async XLA Ops:
  2.1 48.7 %copy-start = (f32[642,512]{1,0:T(8,128)S(1)}, f32[642,512]{1,0:T(8,128)}, u32[]{:S(2)}) copy-start(f32[642,512]{1,0:T(8,128)} %refs_3_.3) | copy-start | bytes 3944452
  2.1 48.7 %copy-start.2 = (f32[256,512]{1,0:T(8,128)S(1)}, f32[256,512]{1,0:T(8,128)}, u32[]{:S(2)}) copy-start(f32[256,512]{1,0:T(8,128)} %refs_1_.2) | copy-start | bytes 1572868
  2.1 48.7 %copy-start.6 = (f32[1024,512]{1,0:T(8,128)S(1)}, f32[1024,512]{1,0:T(8,128)}, u32[]{:S(2)}) copy-start(f32[1024,512]{1,0:T(8,128)} %refs_5_.4) | copy-start | bytes 6291460
  2.1 48.7 %copy-start.8 = (f32[642,512]{1,0:T(8,128)S(1)}, f32[642,512]{1,0:T(8,128)}, u32[]{:S(2)}) copy-start(f32[642,512]{1,0:T(8,128)} %refs_4_.3) | copy-start | bytes 3944452
  2.1 48.7 %copy-start.9 = (f32[512,512]{1,0:T(8,128)S(1)}, f32[512,512]{1,0:T(8,128)}, u32[]{:S(2)}) copy-start(f32[512,512]{1,0:T(8,128)} %refs_6_.3) | copy-start | bytes 3145732
  2.1 48.7 %copy-start.10 = (f32[256,512]{1,0:T(8,128)S(1)}, f32[256,512]{1,0:T(8,128)}, u32[]{:S(2)}) copy-start(f32[256,512]{1,0:T(8,128)} %refs_2_.1) | copy-start | bytes 1572868
  50.9 1.6 copy-start.7
  52.5 42.6 %copy-start.1 = (f32[512,512]{1,0:T(8,128)S(1)}, f32[512,512]{1,0:T(8,128)}, u32[]{:S(2)}) copy-start(f32[512,512]{1,0:T(8,128)} %refs_5_.5) | copy-start | bytes 3145732
  52.5 42.6 %copy-start.3 = (s32[1,1024]{1,0:T(1,128)S(1)}, s32[1,1024]{1,0:T(1,128)}, u32[]{:S(2)}) copy-start(s32[1,1024]{1,0:T(1,128)} %reshape.23.refs_0_.refs_11_) | copy-start | bytes 12292
  52.5 42.6 %copy-start.4 = (s32[1024]{0:T(1024)S(1)}, s32[1024]{0:T(1024)}, u32[]{:S(2)}) copy-start(s32[1024]{0:T(1024)} %param.16) | copy-start | bytes 12292
  52.5 42.6 %copy-start.5 = (s32[1024]{0:T(1024)S(1)}, s32[1024]{0:T(1024)}, u32[]{:S(2)}) copy-start(s32[1024]{0:T(1024)} %param.17) | copy-start | bytes 12292
  52.5 42.6 %copy-start.11 = (f32[1024,128]{1,0:T(8,128)S(1)}, f32[1024,128]{1,0:T(8,128)}, u32[]{:S(2)}) copy-start(f32[1024,128]{1,0:T(8,128)} %get-tuple-element.35.refs_4_) | copy-start | bytes 1572868
  93.4 1.7 copy-start.12
  95.1 44.7 %copy-start.13 = (f32[192,4,8,128]{3,2,1,0:T(8,128)S(1)}, f32[192,4,8,128]{3,2,1,0:T(8,128)}, u32[]{:S(2)}) copy-start(f32[192,4,8,128]{3,2,1,0:T(8,128)} %copy-done.12) | copy-start | bytes 9437188

commit v5 on v4

--- a/solution.py
+++ b/solution.py
@@ -221,6 +221,7 @@
         self.add(part, away, 32, 0)
         self.send_sum(part, 2, away + (1 - spot["two"]) * 16, 16, 64, device)
         self.send_sum(part, 3, away + spot["two"] * 16, 16, 80, device)
+        self.start_kept(part)
 
     def reduce_kept(self, part):
         self.wait(part, 1)
@@ -398,7 +399,6 @@
                 buf[part, position(device, spec), 0] = jnp.zeros((8, 128), F32)
     ring.wait_signals()
     ring.stage("start", *range(4))
-    ring.stage("start_kept", *range(4))
 
     wi, wo = (wi0, wi1), (wo0, wo1)
     fine = NodePass(dot3, wi, wo)
@@ -754,7 +754,6 @@
             row = ROWS
     ring.wait_signals()
     ring.stage("start", *range(LINKS))
-    ring.stage("start_kept", *range(LINKS))
     ring.run(ring.SUM)
 
 

time: 204 us -> 204 us (level)
  no operation moved by 1% of the time
where the time goes in v5:
time: 204 us
  Pallas kernels  198 us (97%)
  local copies, waits for them, and re-layouts  4.77 us (2%)
    pallas_call x3, Pallas kernels, remote_call(): pl.pallas_call(kernel, out_shape=outs, in_specs=vmem_specs(len(args)), ou...  145 us
    pallas_call x1, Pallas kernels, per_device(): pl.pallas_call(front_kernel, out_shape=[wide, wide, wide, rep_out, wide],...  48.7 us
    pallas_call x1, Pallas kernels, finish(): pl.pallas_call(functools.partial(finish_kernel, pieces), out_shape=[f32_o...  4.28 us
    unnamed x29, local copies, waits for them, and re-layouts  4.08 us

profile of v5, /device:TPU:1, one launch (start us, length us, event | category | flops | bytes accessed | tf_op | source)
XLA Modules:
  0.0 203.9 jit_solution(5373931719445004005)
XLA Ops:
  0.6 0.8 copy.21
  1.4 0.7 reshape.23.refs_0_.refs_11_
  2.1 0.0 copy-start
  2.1 0.0 copy-start.2
  2.1 0.0 copy-start.6
  2.1 0.0 copy-start.8
  2.1 0.0 copy-start.9
  2.1 0.0 copy-start.10
  2.1 48.7 %shard_map.180 = (f32[1024,512]{1,0:T(8,128)}, f32[1024,512]{1,0:T(8,128)}, f32[1024,512]{1,0:T(8,128)}, f32[1024,128]{1,0:T(8,128)}, f32[1024,512]{1,0:T(8,128)}) custom-call(s32[1,1024]{1,0:T(1,128)} %reshape.23.refs_0_.refs_11_, s32[1,1024]{1,0:T(1,128)} %bitcast.2, s32[1,1024]{1,0:T(1,128)} %bitcast.4, f32[256,512]{1,0:T(8,128)} %refs_1_.2, ...), custom_call_target="tpu_custom_call" | custom-call | tf_op jit(solution)/shard_map/pallas_call | solution.py:843
  50.8 0.0 copy-done
  50.8 0.0 copy-done.2
  50.8 0.0 copy-done.6
  50.9 0.0 copy-done.8
  50.9 0.0 copy-done.9
  50.9 0.0 copy-done.10
  50.9 0.0 copy-start.7
  50.9 1.6 copy-done.7
  52.5 0.0 copy-start.1
  52.5 0.0 copy-start.3
  52.5 0.0 copy-start.4
  52.5 0.0 copy-start.5
  52.5 0.0 copy-start.11
  52.5 40.9 %shard_map.181 = (f32[1024,512]{1,0:T(8,128)S(1)}, f32[256,512]{1,0:T(8,128)S(1)}, f32[4,8,128]{2,1,0:T(8,128)S(1)}, f32[192,4,8,128]{3,2,1,0:T(8,128)S(1)}) custom-call(f32[1024,512]{1,0:T(8,128)S(1)} %copy-done.7, f32[256,512]{1,0:T(8,128)S(1)} %copy-done.2, f32[256,512]{1,0:T(8,128)S(1)} %copy-done.10, f32[642,512]{1,0:T(8,128)S(1)} %copy-done, ...), custom_call_target="tpu_custom_call" | custom-call | flops 30000001024 | bytes 30000000 | tf_op jit(solution)/shard_map/pallas_call | solution.py:340
  93.4 0.0 copy-start.12
  93.4 1.7 copy-done.12
  95.1 0.0 copy-done.1
  95.1 0.0 copy-done.3
  95.1 0.0 copy-done.4
  95.1 0.0 copy-done.5
  95.1 0.0 copy-done.11
  95.1 0.0 copy-start.13
  95.1 44.6 %shard_map.182 = (f32[1024,512]{1,0:T(8,128)S(1)}, f32[256,512]{1,0:T(8,128)S(1)}, f32[64,4,8,128]{3,2,1,0:T(8,128)S(1)}, f32[64,4,8,128]{3,2,1,0:T(8,128)S(1)},...) custom-call(f32[1024,512]{1,0:T(8,128)S(1)} %get-tuple-element.32.refs_0_, ...), custom_call_target="tpu_custom_call" | custom-call | flops 30000001024 | bytes 30000000 | tf_op jit(solution)/shard_map/pallas_call | solution.py:340
  139.7 0.0 copy-done.13
  139.8 59.7 %shard_map.183.sum_ref = f32[6,128,3,8,128]{4,3,2,1,0:T(8,128)S(1)} custom-call(f32[192,4,8,128]{3,2,1,0:T(8,128)S(1)} %copy-done.13, f32[64,4,8,128]{3,2,1,0:T(8,128)S(1)} %get-tuple-element.38.refs_1_, f32[64,4,8,128]{3,2,1,0:T(8,128)S(1)} %get-tuple-element.39.refs_2_, f32[64,4,8,128]{3,2,1,0:T(8,128)S(1)} %get-tuple-element.40.refs_3_, ...), custom_call_target="tpu_custom_call" | custom-call | flops 30000001024 | bytes 30000000 | tf_op jit(solution)/shard_map/pallas_call | solution.py:340
  199.4 4.3 %shard_map.184 = (f32[642,512]{1,0:T(8,128)}, f32[1536,512]{1,0:T(8,128)}, f32[512,512]{1,0:T(8,128)}, f32[1024,512]{1,0:T(8,128)}, f32[512,512]{1,0:T(8,128)}, /*index=5*/f32[1024,512]{1,0:T(8,128)}, f32[256,512]{1,0:T(8,128)}) custom-call(f32[6,128,3,8,128]{4,3,2,1,0:T(8,128)S(1)} %shard_map.183.sum_ref, f32[1024,512]{1,0:T(8,128)S(1)} %get-tuple-element.44.edges_ref, ...), custom_call_target="tpu_custom_call" | custom-call | tf_op jit(solution)/shard_map/pallas_call | solution.py:801
Async XLA Ops:
  2.1 48.7 %copy-start = (f32[642,512]{1,0:T(8,128)S(1)}, f32[642,512]{1,0:T(8,128)}, u32[]{:S(2)}) copy-start(f32[642,512]{1,0:T(8,128)} %refs_3_.3) | copy-start | bytes 3944452
  2.1 48.7 %copy-start.2 = (f32[256,512]{1,0:T(8,128)S(1)}, f32[256,512]{1,0:T(8,128)}, u32[]{:S(2)}) copy-start(f32[256,512]{1,0:T(8,128)} %refs_1_.2) | copy-start | bytes 1572868
  2.1 48.7 %copy-start.6 = (f32[1024,512]{1,0:T(8,128)S(1)}, f32[1024,512]{1,0:T(8,128)}, u32[]{:S(2)}) copy-start(f32[1024,512]{1,0:T(8,128)} %refs_5_.4) | copy-start | bytes 6291460
  2.1 48.7 %copy-start.8 = (f32[642,512]{1,0:T(8,128)S(1)}, f32[642,512]{1,0:T(8,128)}, u32[]{:S(2)}) copy-start(f32[642,512]{1,0:T(8,128)} %refs_4_.3) | copy-start | bytes 3944452
  2.1 48.7 %copy-start.9 = (f32[512,512]{1,0:T(8,128)S(1)}, f32[512,512]{1,0:T(8,128)}, u32[]{:S(2)}) copy-start(f32[512,512]{1,0:T(8,128)} %refs_6_.3) | copy-start | bytes 3145732
  2.1 48.7 %copy-start.10 = (f32[256,512]{1,0:T(8,128)S(1)}, f32[256,512]{1,0:T(8,128)}, u32[]{:S(2)}) copy-start(f32[256,512]{1,0:T(8,128)} %refs_2_.1) | copy-start | bytes 1572868
  50.9 1.6 copy-start.7
  52.5 42.6 %copy-start.1 = (f32[512,512]{1,0:T(8,128)S(1)}, f32[512,512]{1,0:T(8,128)}, u32[]{:S(2)}) copy-start(f32[512,512]{1,0:T(8,128)} %refs_5_.5) | copy-start | bytes 3145732
  52.5 42.6 %copy-start.3 = (s32[1,1024]{1,0:T(1,128)S(1)}, s32[1,1024]{1,0:T(1,128)}, u32[]{:S(2)}) copy-start(s32[1,1024]{1,0:T(1,128)} %reshape.23.refs_0_.refs_11_) | copy-start | bytes 12292
  52.5 42.6 %copy-start.4 = (s32[1024]{0:T(1024)S(1)}, s32[1024]{0:T(1024)}, u32[]{:S(2)}) copy-start(s32[1024]{0:T(1024)} %param.16) | copy-start | bytes 12292
  52.5 42.6 %copy-start.5 = (s32[1024]{0:T(1024)S(1)}, s32[1024]{0:T(1024)}, u32[]{:S(2)}) copy-start(s32[1024]{0:T(1024)} %param.17) | copy-start | bytes 12292
  52.5 42.6 %copy-start.11 = (f32[1024,128]{1,0:T(8,128)S(1)}, f32[1024,128]{1,0:T(8,128)}, u32[]{:S(2)}) copy-start(f32[1024,128]{1,0:T(8,128)} %get-tuple-element.35.refs_4_) | copy-start | bytes 1572868
  93.4 1.7 copy-start.12
  95.1 44.7 %copy-start.13 = (f32[192,4,8,128]{3,2,1,0:T(8,128)S(1)}, f32[192,4,8,128]{3,2,1,0:T(8,128)}, u32[]{:S(2)}) copy-start(f32[192,4,8,128]{3,2,1,0:T(8,128)} %copy-done.12) | copy-start | bytes 9437188

commit v6 on v4

--- a/solution.py
+++ b/solution.py
@@ -239,7 +239,7 @@
         axis = (self.specs[part][0] + 1) % 3
         self.wait(part, 3, 4)
         self.add(part, spot["second"], 16, 80, 96)
-        for shift in (1, 2, 3):
+        for shift in (2, 1, 3):
             at = spot["second"] + (self.places[axis] + shift) % 4 * 4
             self.send_sum(part, 4 + shift, at, 4, 108 + 4 * shift, self.peer(axis, shift))
 
@@ -248,7 +248,7 @@
         axis = (self.specs[part][0] + 2) % 3
         self.wait(part, 5, 6, 7)
         self.add(part, spot["third"], 4, 112, 116, 120)
-        for shift in (1, 2, 3):
+        for shift in (2, 1, 3):
             at = spot["third"] + (self.places[axis] + shift) % 4
             self.send_sum(part, 7 + shift, at, 1, 123 + shift, self.peer(axis, shift))
 
@@ -258,13 +258,13 @@
 
     def gather_fourth(self, part):
         axis = (self.specs[part][0] + 2) % 3
-        for shift in (1, 2, 3):
+        for shift in (2, 1, 3):
             self.send_block(part, 10 + shift, self.spot[part]["last"], 1, self.peer(axis, shift))
 
     def gather_third(self, part):
         axis = (self.specs[part][0] + 1) % 3
         self.wait(part, 11, 12, 13)
-        for shift in (1, 2, 3):
+        for shift in (2, 1, 3):
             self.send_block(part, 13 + shift, self.spot[part]["third"], 4, self.peer(axis, shift))
 
     def gather_second(self, part):

time: 204 us -> 203 us (level)
  no operation moved by 1% of the time
where the time goes in v6:
time: 203 us
  Pallas kernels  197 us (97%)
  local copies, waits for them, and re-layouts  4.77 us (2%)
    pallas_call x3, Pallas kernels, remote_call(): pl.pallas_call(kernel, out_shape=outs, in_specs=vmem_specs(len(args)), ou...  144 us
    pallas_call x1, Pallas kernels, per_device(): pl.pallas_call(front_kernel, out_shape=[wide, wide, wide, rep_out, wide],...  48.7 us
    pallas_call x1, Pallas kernels, finish(): pl.pallas_call(functools.partial(finish_kernel, pieces), out_shape=[f32_o...  4.28 us
    unnamed x29, local copies, waits for them, and re-layouts  4.08 us

profile of v6, /device:TPU:1, one launch (start us, length us, event | category | flops | bytes accessed | tf_op | source)
XLA Modules:
  0.0 202.7 jit_solution(15764870389336955464)
XLA Ops:
  0.6 0.8 copy.21
  1.4 0.7 reshape.23.refs_0_.refs_11_
  2.1 0.0 copy-start
  2.1 0.0 copy-start.2
  2.1 0.0 copy-start.6
  2.1 0.0 copy-start.8
  2.1 0.0 copy-start.9
  2.1 0.0 copy-start.10
  2.1 48.7 %shard_map.180 = (f32[1024,512]{1,0:T(8,128)}, f32[1024,512]{1,0:T(8,128)}, f32[1024,512]{1,0:T(8,128)}, f32[1024,128]{1,0:T(8,128)}, f32[1024,512]{1,0:T(8,128)}) custom-call(s32[1,1024]{1,0:T(1,128)} %reshape.23.refs_0_.refs_11_, s32[1,1024]{1,0:T(1,128)} %bitcast.2, s32[1,1024]{1,0:T(1,128)} %bitcast.4, f32[256,512]{1,0:T(8,128)} %refs_1_.2, ...), custom_call_target="tpu_custom_call" | custom-call | tf_op jit(solution)/shard_map/pallas_call | solution.py:844
  50.8 0.0 copy-done
  50.8 0.0 copy-done.2
  50.8 0.0 copy-done.6
  50.9 0.0 copy-done.8
  50.9 0.0 copy-done.9
  50.9 0.0 copy-done.10
  50.9 0.0 copy-start.7
  50.9 1.6 copy-done.7
  52.5 0.0 copy-start.1
  52.5 0.0 copy-start.3
  52.5 0.0 copy-start.4
  52.5 0.0 copy-start.5
  52.5 0.0 copy-start.11
  52.5 40.7 %shard_map.181 = (f32[1024,512]{1,0:T(8,128)S(1)}, f32[256,512]{1,0:T(8,128)S(1)}, f32[4,8,128]{2,1,0:T(8,128)S(1)}, f32[192,4,8,128]{3,2,1,0:T(8,128)S(1)}) custom-call(f32[1024,512]{1,0:T(8,128)S(1)} %copy-done.7, f32[256,512]{1,0:T(8,128)S(1)} %copy-done.2, f32[256,512]{1,0:T(8,128)S(1)} %copy-done.10, f32[642,512]{1,0:T(8,128)S(1)} %copy-done, ...), custom_call_target="tpu_custom_call" | custom-call | flops 30000001024 | bytes 30000000 | tf_op jit(solution)/shard_map/pallas_call | solution.py:339
  93.2 0.0 copy-start.12
  93.2 1.7 copy-done.12
  94.8 0.0 copy-done.1
  94.8 0.0 copy-done.3
  94.8 0.0 copy-done.4
  94.8 0.0 copy-done.5
  94.8 0.0 copy-done.11
  94.9 0.0 copy-start.13
  94.9 45.1 %shard_map.182 = (f32[1024,512]{1,0:T(8,128)S(1)}, f32[256,512]{1,0:T(8,128)S(1)}, f32[64,4,8,128]{3,2,1,0:T(8,128)S(1)}, f32[64,4,8,128]{3,2,1,0:T(8,128)S(1)},...) custom-call(f32[1024,512]{1,0:T(8,128)S(1)} %get-tuple-element.32.refs_0_, ...), custom_call_target="tpu_custom_call" | custom-call | flops 30000001024 | bytes 30000000 | tf_op jit(solution)/shard_map/pallas_call | solution.py:339
  140.0 0.0 copy-done.13
  140.0 58.2 %shard_map.183.sum_ref = f32[6,128,3,8,128]{4,3,2,1,0:T(8,128)S(1)} custom-call(f32[192,4,8,128]{3,2,1,0:T(8,128)S(1)} %copy-done.13, f32[64,4,8,128]{3,2,1,0:T(8,128)S(1)} %get-tuple-element.38.refs_1_, f32[64,4,8,128]{3,2,1,0:T(8,128)S(1)} %get-tuple-element.39.refs_2_, f32[64,4,8,128]{3,2,1,0:T(8,128)S(1)} %get-tuple-element.40.refs_3_, ...), custom_call_target="tpu_custom_call" | custom-call | flops 30000001024 | bytes 30000000 | tf_op jit(solution)/shard_map/pallas_call | solution.py:339
  198.2 4.3 %shard_map.184 = (f32[642,512]{1,0:T(8,128)}, f32[1536,512]{1,0:T(8,128)}, f32[512,512]{1,0:T(8,128)}, f32[1024,512]{1,0:T(8,128)}, f32[512,512]{1,0:T(8,128)}, /*index=5*/f32[1024,512]{1,0:T(8,128)}, f32[256,512]{1,0:T(8,128)}) custom-call(f32[6,128,3,8,128]{4,3,2,1,0:T(8,128)S(1)} %shard_map.183.sum_ref, f32[1024,512]{1,0:T(8,128)S(1)} %get-tuple-element.44.edges_ref, ...), custom_call_target="tpu_custom_call" | custom-call | tf_op jit(solution)/shard_map/pallas_call | solution.py:802
Async XLA Ops:
  2.1 48.7 %copy-start = (f32[642,512]{1,0:T(8,128)S(1)}, f32[642,512]{1,0:T(8,128)}, u32[]{:S(2)}) copy-start(f32[642,512]{1,0:T(8,128)} %refs_3_.3) | copy-start | bytes 3944452
  2.1 48.7 %copy-start.2 = (f32[256,512]{1,0:T(8,128)S(1)}, f32[256,512]{1,0:T(8,128)}, u32[]{:S(2)}) copy-start(f32[256,512]{1,0:T(8,128)} %refs_1_.2) | copy-start | bytes 1572868
  2.1 48.7 %copy-start.6 = (f32[1024,512]{1,0:T(8,128)S(1)}, f32[1024,512]{1,0:T(8,128)}, u32[]{:S(2)}) copy-start(f32[1024,512]{1,0:T(8,128)} %refs_5_.4) | copy-start | bytes 6291460
  2.1 48.7 %copy-start.8 = (f32[642,512]{1,0:T(8,128)S(1)}, f32[642,512]{1,0:T(8,128)}, u32[]{:S(2)}) copy-start(f32[642,512]{1,0:T(8,128)} %refs_4_.3) | copy-start | bytes 3944452
  2.1 48.7 %copy-start.9 = (f32[512,512]{1,0:T(8,128)S(1)}, f32[512,512]{1,0:T(8,128)}, u32[]{:S(2)}) copy-start(f32[512,512]{1,0:T(8,128)} %refs_6_.3) | copy-start | bytes 3145732
  2.1 48.7 %copy-start.10 = (f32[256,512]{1,0:T(8,128)S(1)}, f32[256,512]{1,0:T(8,128)}, u32[]{:S(2)}) copy-start(f32[256,512]{1,0:T(8,128)} %refs_2_.1) | copy-start | bytes 1572868
  50.9 1.6 copy-start.7
  52.5 42.4 %copy-start.1 = (f32[512,512]{1,0:T(8,128)S(1)}, f32[512,512]{1,0:T(8,128)}, u32[]{:S(2)}) copy-start(f32[512,512]{1,0:T(8,128)} %refs_5_.5) | copy-start | bytes 3145732
  52.5 42.4 %copy-start.3 = (s32[1,1024]{1,0:T(1,128)S(1)}, s32[1,1024]{1,0:T(1,128)}, u32[]{:S(2)}) copy-start(s32[1,1024]{1,0:T(1,128)} %reshape.23.refs_0_.refs_11_) | copy-start | bytes 12292
  52.5 42.4 %copy-start.4 = (s32[1024]{0:T(1024)S(1)}, s32[1024]{0:T(1024)}, u32[]{:S(2)}) copy-start(s32[1024]{0:T(1024)} %param.16) | copy-start | bytes 12292
  52.5 42.4 %copy-start.5 = (s32[1024]{0:T(1024)S(1)}, s32[1024]{0:T(1024)}, u32[]{:S(2)}) copy-start(s32[1024]{0:T(1024)} %param.17) | copy-start | bytes 12292
  52.5 42.4 %copy-start.11 = (f32[1024,128]{1,0:T(8,128)S(1)}, f32[1024,128]{1,0:T(8,128)}, u32[]{:S(2)}) copy-start(f32[1024,128]{1,0:T(8,128)} %get-tuple-element.35.refs_4_) | copy-start | bytes 1572868
  93.2 1.7 copy-start.12
  94.9 45.2 %copy-start.13 = (f32[192,4,8,128]{3,2,1,0:T(8,128)S(1)}, f32[192,4,8,128]{3,2,1,0:T(8,128)}, u32[]{:S(2)}) copy-start(f32[192,4,8,128]{3,2,1,0:T(8,128)} %copy-done.12) | copy-start | bytes 9437188
